TPU v7x, 256 devices: a whole 4x4x8 slice. The times are simulated.
256 devices in a mesh: dp: 8 (over z), cls: 8 (over y, core), feat: 4 (over x).
Axes of the slice: x: 4, y: 4, z: 8, core: 2. Of those that a mesh axis runs over, the one named last changes fastest.
Arguments:
- utter: bfloat16 [65536, 1024], P(('dp', 'cls'), 'feat'), may hold values from -6 to 6
- intents: bfloat16 [524288, 1024], P(('dp', 'cls'), 'feat'), may hold values from -0.1875 to 0.1875
- req_blocks: int32 [512, 16], replicated, may hold values from -1 to 4095, as said below
- req_count: int32 [512], replicated, may hold values from 4 to 16, as said below
- block_home: int32 [4096], replicated, may hold values from 0 to 4095, as said below
- labels: int32 [65536, 2], P(('dp', 'cls')), may hold values from 0 to 524287, as said below
Outputs:
- grad_utter: bfloat16 [65536, 1024], P(('dp', 'cls'), 'feat')
- grad_intents: bfloat16 [524288, 1024], P(('dp', 'cls'), 'feat')
Inputs may be any that keep to these rules, and one draw needn't show every extreme that they name: `req_blocks`: on each device along dp+cls the live entries of its 8 lists are distinct blocks, and at most 2 of them have block_home within one device's range of 64 stored blocks; entries at or past req_count are -1. `req_count`: the 8 counts of one device sum to 64. `block_home`: A permutation of the block ids. `labels`: each label lies in a live block of its utterance block's list.
All inputs are finite; a program needn't handle non-finite values.
Results may differ from a plain program's by a relative error of at most 0.0052.
Values may be sent and summed in bfloat16 or wider, within the bound.
A program may use at most 128 MiB of HBM per device.

v0:
```python
import jax
import jax.numpy as jnp
from jax import lax
from jax.sharding import PartitionSpec as P

BLK = 128
BLK_DEV = 64
UB = 128
UBD = 8
MOST = 16
REQ_DEV = 64


GAMMA = 4.0
MARGIN = 0.25


def slope_blocks(scores, blocks, live_count, label_ids):
    list_len = blocks.shape[1]
    block_width = scores.shape[3]
    cand_ids = blocks[:, :, None] * block_width + jnp.arange(block_width)[None, None, :]
    target = jnp.zeros(scores.shape, jnp.bool_)
    for label_pos in range(label_ids.shape[2]):
        target = target | (cand_ids[:, :, None, :] == label_ids[:, None, :, label_pos, None])
    target = target.astype(jnp.float32)
    alive = (jnp.arange(list_len)[None, :] < live_count[:, None]).astype(jnp.float32)
    logits = GAMMA * scores
    derivative = (1.0 - target) * jax.nn.sigmoid(logits + MARGIN) - target * jax.nn.sigmoid(
        MARGIN - logits
    )
    return (
        GAMMA
        * alive[:, :, None, None]
        * derivative
        / live_count.astype(jnp.float32)[:, None, None, None]
    ).astype(jnp.bfloat16)


def shards(utter, intents, req_blocks, req_count, block_home, labels):
    owners = lax.axis_size(("dp", "cls"))
    own_index = lax.axis_index(("dp", "cls"))
    part_width = intents.shape[1]
    capacity = 2 * REQ_DEV // owners
    entries = UBD * MOST
    slot_count = capacity * owners
    live_all = jnp.arange(MOST)[None, :] < req_count[:, None]
    home_all = block_home[jnp.maximum(req_blocks, 0)]
    owner_all = jnp.where(live_all, home_all // BLK_DEV, -1).reshape(owners, entries)
    local_all = (home_all % BLK_DEV).reshape(owners, entries)
    earlier = jnp.arange(entries)[:, None] > jnp.arange(entries)[None, :]
    rank_all = jnp.sum((owner_all[:, :, None] == owner_all[:, None, :]) & earlier[None], axis=2)
    wanted = (owner_all[:, :, None] == own_index) & (
        rank_all[:, :, None] == jnp.arange(capacity)[None, None, :]
    )
    present = jnp.any(wanted, axis=1)
    local_for = jnp.sum(jnp.where(wanted, local_all[:, :, None], 0), axis=1)
    stored = intents.reshape(BLK_DEV, BLK, part_width)
    outgoing = jnp.where(present[:, :, None, None], stored[local_for], jnp.zeros((), intents.dtype))
    incoming = lax.all_to_all(outgoing, ("dp", "cls"), split_axis=0, concat_axis=0, tiled=True)
    incoming = incoming.reshape(slot_count, BLK, part_width)
    my_owner = lax.dynamic_index_in_dim(owner_all, own_index, 0, keepdims=False)
    my_rank = lax.dynamic_index_in_dim(rank_all, own_index, 0, keepdims=False)
    my_dest = jnp.where(my_owner >= 0, my_owner * capacity + my_rank, -1)
    fetched_lists = incoming[jnp.maximum(my_dest, 0)].reshape(UBD, MOST * BLK, part_width)
    my_blocks = lax.dynamic_slice_in_dim(req_blocks, own_index * UBD, UBD, 0)
    my_count = lax.dynamic_slice_in_dim(req_count, own_index * UBD, UBD, 0)
    row_blocks = utter.reshape(UBD, UB, part_width)
    label_ids = labels.reshape(UBD, UB, labels.shape[1])
    list_blocks = fetched_lists.reshape(UBD, MOST, BLK, part_width)
    partial_sum = jnp.einsum(
        "bud,bmcd->bmuc", row_blocks, list_blocks, preferred_element_type=jnp.float32
    ).reshape(entries, UB, BLK)
    position = jnp.arange(MOST)
    starts = jnp.cumsum(my_count) - my_count
    live_mine = (position[None, :] < my_count[:, None]).reshape(entries)
    slot_of = jnp.where(live_mine, (starts[:, None] + position[None, :]).reshape(entries), REQ_DEV)
    pick_map = slot_of[None, :] == jnp.arange(REQ_DEV)[:, None]
    pick_from = jnp.sum(jnp.where(pick_map, jnp.arange(entries)[None, :], 0), axis=1)
    packed = partial_sum[pick_from]
    summed_live = lax.psum(packed, "feat")
    scores = summed_live[jnp.minimum(slot_of, REQ_DEV - 1)].reshape(UBD, MOST, UB, BLK)
    grad_scores = slope_blocks(scores, my_blocks, my_count, label_ids)
    grad_rows = jnp.einsum(
        "bmuc,bmcd->bud", grad_scores, list_blocks, preferred_element_type=jnp.float32
    ).astype(jnp.bfloat16)
    grad_lists = jnp.einsum(
        "bmuc,bud->bmcd", grad_scores, row_blocks, preferred_element_type=jnp.float32
    ).astype(jnp.bfloat16)
    contrib = grad_lists.reshape(entries, BLK, part_width)
    hit_map = my_dest[None, :] == jnp.arange(slot_count)[:, None]
    source = jnp.sum(jnp.where(hit_map, jnp.arange(entries)[None, :], 0), axis=1)
    filled = jnp.any(hit_map, axis=1)
    back_out = jnp.where(
        filled[:, None, None], contrib[source], jnp.zeros((), jnp.bfloat16)
    ).reshape(owners, capacity, BLK, part_width)
    returned = lax.all_to_all(back_out, ("dp", "cls"), split_axis=0, concat_axis=0, tiled=True)
    placing = (
        local_for.reshape(slot_count)[None, :] == jnp.arange(BLK_DEV)[:, None]
    ) & present.reshape(slot_count)[None, :]
    summed = jnp.dot(
        placing.astype(jnp.bfloat16),
        returned.reshape(slot_count, BLK * part_width),
        preferred_element_type=jnp.float32,
    )
    grad_intents = summed.astype(jnp.bfloat16).reshape(BLK_DEV * BLK, part_width)
    grad_utter = grad_rows.reshape(UBD * UB, part_width)
    return (grad_utter, grad_intents)


def solution(mesh):
    return jax.shard_map(
        shards,
        mesh=mesh,
        in_specs=(
            P(("dp", "cls"), "feat"),
            P(("dp", "cls"), "feat"),
            P(),
            P(),
            P(),
            P(("dp", "cls"), None),
        ),
        out_specs=(P(("dp", "cls"), "feat"), P(("dp", "cls"), "feat")),
        check_vma=False,
    )
```

profile of v0, /device:TPU:64, one launch (start us, length us, event | category | flops | bytes accessed | tf_op | source)
XLA Modules:
  0.0 661.2 jit_solution(7270448650649260813)
XLA Ops:
  7.2 0.8 broadcast_maximum_fusion
  9.4 45.5 %gather_fusion = s32[8192]{0:T(1024)S(1)} fusion(s32[4096]{0:T(1024)S(1)} %copy-done.1, s32[8192]{0:T(1024)S(1)} %broadcast_clamp_fusion), kind=kCustom, calls=%fused_computation | custom fusion | bytes 98304 | tf_op jit(solution)/shard_map/gather | solution.py:47
  55.1 2.6 convert_reduce_fusion
  58.2 8.7 %gather_fusion.1 = bf16[128,128,256]{2,1,0:T(8,128)(2,1)} fusion(bf16[64,128,256]{2,1,0:T(8,128)(2,1)} %bitcast.107, s32[1024]{0:T(1024)S(1)} %pad_clamp_fusion.4), kind=kCustom, calls=%fused_computation.1 | custom fusion | bytes 16777728 | tf_op jit(solution)/shard_map/gather | solution.py:58
  66.9 7.2 %broadcast_select_fusion.1 = bf16[64,2,128,256]{3,2,1,0:T(8,128)(2,1)} fusion(bf16[64,2,128,256]{3,2,1,0:T(8,128)(2,1)} %bitcast.106, pred[64,2]{1,0:T(8,128)(4,1)S(1)} %copy.53), kind=kLoop, calls=%fused_computation.11 | loop fusion | flops 4194304 | bytes 16777344 | tf_op jit(solution)/shard_map/jit(_where)/select_n | solution.py:58
  74.1 11.5 %all-to-all-start = ((bf16[64,2,128,256]{3,2,1,0:T(8,128)(2,1)}), bf16[64,2,128,256]{3,2,1,0:T(8,128)(2,1)}, u32[]{:S(2)}, u32[]{:S(2)}) async-start(bf16[64,2,128,256]{3,2,1,0:T(8,128)(2,1)} %broadcast_select_fusion.1), calls=%async_computation | async-start | bytes 16777216 | tf_op jit(solution)/shard_map/all_to_all | solution.py:59
  87.3 182.5 %all-to-all-done = bf16[64,2,128,256]{3,2,1,0:T(8,128)(2,1)} async-done(((bf16[64,2,128,256]{3,2,1,0:T(8,128)(2,1)}), bf16[64,2,128,256]{3,2,1,0:T(8,128)(2,1)}, u32[]{:S(2)}, u32[]{:S(2)}) %all-to-all-start) | async-done | bytes 8388640 | tf_op jit(solution)/shard_map/all_to_all | solution.py:59
  269.8 9.8 %gather_fusion.2 = bf16[128,128,256]{2,1,0:T(8,128)(2,1)} fusion(bf16[128,128,256]{2,1,0:T(8,128)(2,1)} %bitcast.7, s32[1024]{0:T(1024)S(1)} %pad_clamp_fusion.3), kind=kCustom, calls=%fused_computation.2 | custom fusion | bytes 16777728 | tf_op jit(solution)/shard_map/gather | solution.py:64
  279.6 8.9 %fusion.17 = f32[8,16,128,128]{3,2,1,0:T(8,128)} fusion(bf16[8,16,128,256]{3,2,1,0:T(8,128)(2,1)} %bitcast.98, bf16[8,128,256,1]{2,1,3,0:T(8,128)(2,1)S(1)} %bitcast.96), kind=kOutput, calls=%fused_computation.74 | convolution fusion | flops 1073741824 | bytes 17301504 | tf_op jit(solution)/shard_map/bud,bmcd->bmuc/dot_general | solution.py:70
  288.6 6.2 gather_fusion.3
  296.4 95.6 %all-reduce.2.cloned.1.call-done = f32[64,128,128]{1,2,0:T(8,128)} async-done(((f32[64,128,128]{1,2,0:T(8,128)}), f32[64,128,128]{1,2,0:T(8,128)}) %all-reduce.2.cloned.1.call-update) | async-done | bytes 4194320 | tf_op jit(solution)/shard_map/psum | solution.py:80
  392.0 6.5 gather_fusion.4
  398.5 6.6 add_divide_fusion.1
  405.0 3.6 divide_convert_fusion
  408.7 2.0 copy-done.2
  410.7 5.6 convolution_convert_fusion.1
  416.2 9.8 %gather_fusion.5 = bf16[128,128,256]{2,1,0:T(8,128)(2,1)} fusion(bf16[128,128,256]{2,1,0:T(8,128)(2,1)} %bitcast.103, s32[1024]{0:T(1024)S(1)} %pad_clamp_fusion), kind=kCustom, calls=%fused_computation.5 | custom fusion | bytes 16777728 | tf_op jit(solution)/shard_map/gather | solution.py:94
  426.1 7.2 %broadcast_select_fusion = bf16[64,2,128,256]{3,2,1,0:T(8,128)(2,1)} fusion(bf16[64,2,128,256]{3,2,1,0:T(8,128)(2,1)} %bitcast.104, pred[64,2]{1,0:T(8,128)(4,1)S(1)} %broadcast_in_dim.115), kind=kLoop, calls=%fused_computation.10 | loop fusion | flops 4194304 | bytes 16777344 | tf_op jit(solution)/shard_map/jit(_where)/select_n | solution.py:93
  433.3 10.6 %all-to-all-start.1 = ((bf16[64,2,128,256]{3,2,1,0:T(8,128)(2,1)}), bf16[64,2,128,256]{3,2,1,0:T(8,128)(2,1)}, u32[]{:S(2)}, u32[]{:S(2)}) async-start(bf16[64,2,128,256]{3,2,1,0:T(8,128)(2,1)} %broadcast_select_fusion), calls=%async_computation.1 | async-start | bytes 16777216 | tf_op jit(solution)/shard_map/all_to_all | solution.py:96
  444.3 7.1 %fusion = bf16[8,128,256]{2,1,0:T(8,128)(2,1)} fusion(bf16[8,16,128,128]{2,3,1,0:T(8,128)(2,1)} %copy-done.2, bf16[8,16,128,256]{3,2,1,0:T(8,128)(2,1)} %bitcast.99), kind=kOutput, calls=%fused_computation.15 | convolution fusion | flops 1074003968 | bytes 13107200 | tf_op jit(solution)/shard_map/bmuc,bmcd->bud/dot_general | solution.py:83
  451.3 176.7 %all-to-all-done.1 = bf16[64,2,128,256]{3,2,1,0:T(8,128)(2,1)} async-done(((bf16[64,2,128,256]{3,2,1,0:T(8,128)(2,1)}), bf16[64,2,128,256]{3,2,1,0:T(8,128)(2,1)}, u32[]{:S(2)}, u32[]{:S(2)}) %all-to-all-start.1) | async-done | bytes 8388640 | tf_op jit(solution)/shard_map/all_to_all | solution.py:96
  628.1 12.3 %copy.63 = bf16[16,8,128,256]{3,1,2,0:T(8,128)(2,1)} copy(bf16[16,8,128,256]{3,2,1,0:T(8,128)(2,1)} %bitcast.40) | data formatting | bytes 16777216
  640.4 6.6 convolution_convert_fusion
  647.0 7.4 %reshape.449 = bf16[8192,256]{1,0:T(8,128)(2,1)} reshape(bf16[64,32768]{1,0:T(8,128)(2,1)} %convolution_convert_fusion) | data formatting | bytes 8388608 | tf_op jit(solution)/shard_map/reshape | solution.py:105
  (62 shorter events, 5.6 us)
Async XLA Ops:
  7.2 272.5 %copy-start = (bf16[1024,256]{1,0:T(8,128)(2,1)S(1)}, bf16[1024,256]{1,0:T(8,128)(2,1)}, u32[]{:S(2)}) copy-start(bf16[1024,256]{1,0:T(8,128)(2,1)} %param.6) | copy-start | bytes 1572868
  7.2 2.2 copy-start.1
  74.1 195.7 %all-to-all-start = ((bf16[64,2,128,256]{3,2,1,0:T(8,128)(2,1)}), bf16[64,2,128,256]{3,2,1,0:T(8,128)(2,1)}, u32[]{:S(2)}, u32[]{:S(2)}) async-start(bf16[64,2,128,256]{3,2,1,0:T(8,128)(2,1)} %broadcast_select_fusion.1), calls=%async_computation | async-start | bytes 16777216 | tf_op jit(solution)/shard_map/all_to_all | solution.py:59
  85.6 306.4 %all-reduce.2.cloned.1.call-start = ((), (), s32[]{:S(2)}) async-start(), calls=%async_computation.2 | async-start | bytes 8388608 | tf_op jit(solution)/shard_map/psum | solution.py:80
  288.6 7.3 %copy-start.3 = (s32[1024,2]{0,1:T(2,128)S(1)}, s32[1024,2]{0,1:T(2,128)}, u32[]{:S(2)}) copy-start(s32[1024,2]{0,1:T(2,128)} %param.11) | copy-start | bytes 24580
  408.7 2.0 copy-start.2
  433.3 194.8 %all-to-all-start.1 = ((bf16[64,2,128,256]{3,2,1,0:T(8,128)(2,1)}), bf16[64,2,128,256]{3,2,1,0:T(8,128)(2,1)}, u32[]{:S(2)}, u32[]{:S(2)}) async-start(bf16[64,2,128,256]{3,2,1,0:T(8,128)(2,1)} %broadcast_select_fusion), calls=%async_computation.1 | async-start | bytes 16777216 | tf_op jit(solution)/shard_map/all_to_all | solution.py:96
Sparse Core Ops, SparseCore 0:
  295.0 97.0 all-reduce.1
where the time goes:
time: 665 us; the launch traced here: 661 us
  waiting for transfers between devices  455 us (68%)
  local copies, waits for them, and re-layouts  112 us (17%)
  other arithmetic  29.9 us (4%)
  matrix products  28.2 us (4%)
  starting transfers between devices  22.3 us (3%)
  between operations  14.3 us (2%)
    all_to_all x1, waiting for transfers between devices, shards(): lax.all_to_all(outgoing, ('dp', 'cls'), split_axis=0, concat_axis=0, tile...  183 us
    all_to_all x1, waiting for transfers between devices, shards(): lax.all_to_all(back_out, ('dp', 'cls'), split_axis=0, concat_axis=0, tile...  177 us
    psum x1, waiting for transfers between devices, shards(): summed_live = lax.psum(packed, 'feat')  95.6 us
    gather x1, local copies, waits for them, and re-layouts, shards(): home_all = block_home[jnp.maximum(req_blocks, 0)]  45.5 us
    unnamed x11, local copies, waits for them, and re-layouts  14.4 us
  transfers between devices with their start and end apart: 3, of which 3 were waited for; matrix products, arithmetic and copies ran while one was open for 2% of the time, Pallas kernels for 0%

commit v1 on v0

v1 whole, which is shorter than its diff:
```python
import functools

import jax
import jax.numpy as jnp
import numpy as np
from jax import lax
from jax.experimental import pallas as pl
from jax.experimental.pallas import tpu as pltpu
from jax.sharding import PartitionSpec as P

BLK = 128
BLK_DEV = 64
UB = 128
UBD = 8
MOST = 16
GAMMA = 4.0
MARGIN = 0.25

NY, NZ = 4, 8
CHIPS = NY * NZ
SLOTS = 4
DEPTH = 4
LAG = 3
HALVES = 2
PART = UBD // HALVES
MESH = pl.DeviceIdType.MESH

CYCLES = (
    (0, 8, 9, 1, 25, 24, 16, 17, 18, 10, 2, 26, 27, 19, 11, 3, 4, 12, 20, 28, 29, 5, 13, 21, 22, 30, 6, 14, 15, 23, 31, 7),
    (0, 1, 2, 3, 27, 28, 4, 5, 6, 7, 15, 8, 16, 23, 22, 14, 13, 12, 11, 10, 9, 17, 25, 26, 18, 19, 20, 21, 29, 30, 31, 24),
)


def _tables():
    link = np.zeros((2, CHIPS), np.int64)
    order = np.zeros((CHIPS, 2, CHIPS), np.int32)
    for c, cycle in enumerate(CYCLES):
        for i, chip in enumerate(cycle):
            after, before = cycle[(i + 1) % CHIPS], cycle[(i - 1) % CHIPS]
            link[c, chip] = (after * CHIPS + before) * 2 + i % 2
            for n in range(CHIPS):
                source = cycle[(i - n) % CHIPS] if (i + n) % 2 == 0 else cycle[(i + n) % CHIPS]
                order[chip, c, n] = (source % NZ) * (2 * NY) + (source // NZ) * 2 + c
    return link, order


LINK, ORDER = _tables()


def ring_kernel(
    ku_ref, lb_ref, bid_ref, scale_ref, utter_ref, lab_ref, intents_ref,
    gu_ref, con_ref,
    ag, aglab, rs, w, ucur, usel, labsel, part, recv, gs, gbuf, cst,
    sem_in, sem_w, ag_send, ag_recv, lab_send, lab_recv, rs_send, rs_recv,
    part_send, part_recv, gs_send, gs_recv, con_send, con_recv, con_loc, sem_out,
):
    z = lax.axis_index("dp")
    cl = lax.axis_index("cls")
    x = lax.axis_index("feat")
    y = cl // 2
    core = cl % 2
    chip = y * NZ + z
    code = chip + core * CHIPS
    packed = jnp.int32(0)
    for c in range(2):
        for k in range(CHIPS):
            packed = packed + jnp.where(code == c * CHIPS + k, jnp.int32(int(LINK[c, k])), jnp.int32(0))
    after = packed // (2 * CHIPS)
    before = (packed // 2) % CHIPS
    parity = packed % 2

    def device_of(c):
        return (c % NZ, (c // NZ) * 2 + core, x)

    def down(n):
        odd = (parity + n) % 2
        return device_of(after + odd * (before - after))

    other = (z, y * 2 + (1 - core), x)

    def peer(o):
        return (z, cl, (x + o) % 4)

    def ag_copy(n, h):
        return pltpu.make_async_remote_copy(
            src_ref=ag.at[n, pl.ds(h * PART, PART)], dst_ref=ag.at[n + 1, pl.ds(h * PART, PART)],
            send_sem=ag_send.at[n, h], recv_sem=ag_recv.at[n + 1, h], device_id=down(n), device_id_type=MESH)

    def ag_wait(n, h):
        pltpu.make_async_remote_copy(
            src_ref=ag.at[n, pl.ds(h * PART, PART)], dst_ref=ag.at[n, pl.ds(h * PART, PART)],
            send_sem=ag_send.at[n, h], recv_sem=ag_recv.at[n, h], device_id=down(n), device_id_type=MESH).wait_recv()

    def lab_copy(n):
        return pltpu.make_async_remote_copy(
            src_ref=aglab.at[n], dst_ref=aglab.at[n + 1],
            send_sem=lab_send.at[n], recv_sem=lab_recv.at[n + 1], device_id=down(n), device_id_type=MESH)

    def lab_wait(n):
        pltpu.make_async_remote_copy(
            src_ref=aglab.at[n], dst_ref=aglab.at[n],
            send_sem=lab_send.at[n], recv_sem=lab_recv.at[n], device_id=down(n), device_id_type=MESH).wait_recv()

    def rs_copy(m, h):
        return pltpu.make_async_remote_copy(
            src_ref=rs.at[m - 1, pl.ds(h * PART, PART)], dst_ref=rs.at[m, pl.ds(h * PART, PART)],
            send_sem=rs_send.at[m - 1, h], recv_sem=rs_recv.at[m, h], device_id=down(m), device_id_type=MESH)

    def rs_wait(m, h):
        pltpu.make_async_remote_copy(
            src_ref=rs.at[m - 1, pl.ds(h * PART, PART)], dst_ref=rs.at[m - 1, pl.ds(h * PART, PART)],
            send_sem=rs_send.at[m - 1, h], recv_sem=rs_recv.at[m - 1, h], device_id=down(m), device_id_type=MESH).wait_recv()

    def part_copy(n, o):
        to = (x + o) % 4
        return pltpu.make_async_remote_copy(
            src_ref=part.at[n % DEPTH, to], dst_ref=recv.at[n % DEPTH, o - 1],
            send_sem=part_send.at[n % DEPTH, o - 1], recv_sem=part_recv.at[n % DEPTH, o - 1],
            device_id=peer(o), device_id_type=MESH)

    def gs_copy(m, o):
        return pltpu.make_async_remote_copy(
            src_ref=gs.at[m % DEPTH, x], dst_ref=gs.at[m % DEPTH, x],
            send_sem=gs_send.at[m % DEPTH, o - 1], recv_sem=gs_recv.at[m % DEPTH, o - 1],
            device_id=peer(o), device_id_type=MESH)

    def gs_wait(m, o):
        source = (x + 4 - o) % 4
        pltpu.make_async_remote_copy(
            src_ref=gs.at[m % DEPTH, source], dst_ref=gs.at[m % DEPTH, source],
            send_sem=gs_send.at[m % DEPTH, o - 1], recv_sem=gs_recv.at[m % DEPTH, o - 1],
            device_id=peer(o), device_id_type=MESH).wait_recv()

    def con_far(m):
        return pltpu.make_async_remote_copy(
            src_ref=cst.at[m % DEPTH, pl.ds(2 * (1 - core), 2)], dst_ref=con_ref.at[core, m],
            send_sem=con_send.at[m % DEPTH], recv_sem=con_recv.at[m], device_id=other, device_id_type=MESH)

    def con_far_wait(m):
        pltpu.make_async_remote_copy(
            src_ref=cst.at[m % DEPTH, pl.ds(2 * (1 - core), 2)], dst_ref=con_ref.at[1 - core, m],
            send_sem=con_send.at[m % DEPTH], recv_sem=con_recv.at[m], device_id=other, device_id_type=MESH).wait_recv()

    def con_near(m):
        return pltpu.make_async_copy(
            cst.at[m % DEPTH, pl.ds(2 * core, 2)], con_ref.at[core, m], con_loc.at[m % DEPTH])

    own_u = pltpu.make_async_copy(utter_ref, ag.at[0], sem_in.at[0])
    own_l = pltpu.make_async_copy(lab_ref, aglab.at[0], sem_in.at[1])
    own_w = pltpu.make_async_copy(intents_ref, w.at[pl.ds(core * BLK_DEV, BLK_DEV)], sem_in.at[2])
    far_w = pltpu.make_async_remote_copy(
        src_ref=intents_ref, dst_ref=w.at[pl.ds(core * BLK_DEV, BLK_DEV)],
        send_sem=sem_w.at[0], recv_sem=sem_w.at[1], device_id=other, device_id_type=MESH)
    far_w_in = pltpu.make_async_remote_copy(
        src_ref=intents_ref, dst_ref=w.at[pl.ds((1 - core) * BLK_DEV, BLK_DEV)],
        send_sem=sem_w.at[0], recv_sem=sem_w.at[1], device_id=other, device_id_type=MESH)
    own_u.start()
    own_l.start()
    own_w.start()
    rs[0] = jnp.zeros(rs.shape[1:], rs.dtype)

    barrier = pltpu.get_barrier_semaphore()
    for device in (device_of(after), device_of(before), other, peer(1), peer(2), peer(3)):
        pl.semaphore_signal(barrier, inc=1, device_id=device, device_id_type=MESH)
    pl.semaphore_wait(barrier, 6)
    far_w.start()
    own_u.wait()
    own_l.wait()

    def stage_ag(n, h):
        @pl.when((n >= 1) & (n < CHIPS))
        def _():
            ag_wait(n, h)
            if h == 0:
                lab_wait(n)

        @pl.when(n < CHIPS - 1)
        def _():
            ag_copy(n, h).start()
            if h == 0:
                lab_copy(n).start()

    def stage_rs(m, h):
        @pl.when((m >= 1) & (m <= CHIPS))
        def _():
            @pl.when(m >= 2)
            def _():
                rs_wait(m, h)

            row = m % CHIPS
            slot = jnp.where(row == 0, 2, m % 2)
            kus = [ku_ref[row * SLOTS + s] for s in range(SLOTS)]
            for j in range(h * PART, (h + 1) * PART):
                total = rs[m - 1, j].astype(jnp.float32)
                for s in range(SLOTS):
                    total = total + gbuf[slot, s] * (kus[s] == j).astype(jnp.float32)
                rs[m - 1, j] = total.astype(jnp.bfloat16)

            @pl.when(m < CHIPS)
            def _():
                rs_copy(m, h).start()

    def stage_scores(n):
        @pl.when(n < CHIPS)
        def _():
            d = n % DEPTH

            @pl.when(n >= DEPTH)
            def _():
                for o in range(1, 4):
                    part_copy(n, o).wait_send()

            for j in range(UBD):
                ucur[j] = ag[n, j]
            mine = ku_ref[n * SLOTS + x]
            rows = lax.broadcasted_iota(jnp.int32, (UBD, UB), 0)
            for k in range(2):
                labs = aglab[n, k * UBD:(k + 1) * UBD]
                labsel[d, k:k + 1] = jnp.sum(jnp.where(rows == mine, labs, 0), axis=0, keepdims=True)
            for s in range(SLOTS):
                block = ucur[ku_ref[n * SLOTS + s]]
                usel[d, s] = block
                part[d, s] = lax.dot_general(
                    w[lb_ref[n * SLOTS + s]], block, (((1,), (1,)), ((), ())),
                    preferred_element_type=jnp.float32)
            for o in range(1, 4):
                part_copy(n, o).start()

    def stage_slope(m):
        @pl.when((m >= 0) & (m < CHIPS))
        def _():
            d = m % DEPTH

            @pl.when(m >= DEPTH)
            def _():
                for o in range(1, 4):
                    gs_copy(m, o).wait_send()

            total = part[d, x]
            for o in range(1, 4):
                part_copy(m, o).wait_recv()
                total = total + recv[d, o - 1]
            logits = GAMMA * total
            ids = lax.broadcasted_iota(jnp.int32, (BLK, UB), 0) + bid_ref[m * SLOTS + x] * BLK
            hit = (ids == labsel[d, 0:1]) | (ids == labsel[d, 1:2])
            slope = jax.nn.sigmoid(jnp.where(hit, MARGIN - logits, logits + MARGIN))
            slope = jnp.where(hit, -slope, slope) * scale_ref[m * SLOTS + x]
            gs[d, x] = slope.astype(jnp.bfloat16)
            for o in range(1, 4):
                gs_copy(m, o).start()

    def stage_grads(m):
        @pl.when((m >= 0) & (m < CHIPS))
        def _():
            d = m % DEPTH
            slot = jnp.where(m == 0, 2, m % 2)

            @pl.when(m >= DEPTH)
            def _():
                con_far(m).wait_send()
                con_near(m).wait()

            for o in range(1, 4):
                gs_wait(m, o)
            for s in range(SLOTS):
                slope = gs[d, s]
                cst[d, s] = jnp.dot(slope, usel[d, s], preferred_element_type=jnp.float32).astype(jnp.bfloat16)
                gbuf[slot, s] = lax.dot_general(
                    slope, w[lb_ref[m * SLOTS + s]], (((0,), (0,)), ((), ())),
                    preferred_element_type=jnp.float32)
            con_far(m).start()
            con_near(m).start()

    def step(n, carry):
        for h in range(HALVES):
            stage_ag(n, h)

            @pl.when(n == 0)
            def _():
                if h == 0:
                    own_w.wait()
                    far_w_in.wait_recv()

            stage_rs(n - LAG, h)
        stage_scores(n)
        stage_slope(n - 1)
        stage_grads(n - 2)
        return carry

    lax.fori_loop(0, CHIPS + LAG + 1, step, 0)

    out = pltpu.make_async_copy(rs.at[CHIPS - 1], gu_ref, sem_out)
    out.start()

    def drain(n, carry):
        for h in range(HALVES):
            ag_copy(n, h).wait_send()
            rs_copy(n + 1, h).wait_send()
        lab_copy(n).wait_send()
        con_far_wait(n)
        return carry

    lax.fori_loop(0, CHIPS - 1, drain, 0)
    con_far_wait(CHIPS - 1)
    for n in range(CHIPS - DEPTH, CHIPS):
        for o in range(1, 4):
            part_copy(n, o).wait_send()
            gs_copy(n, o).wait_send()
        con_far(n).wait_send()
        con_near(n).wait()
    far_w.wait_send()
    out.wait()


def ring(ku, lb, bid, scale, utter, labs, intents):
    width = intents.shape[2]
    block = (UB, width)
    dma = pltpu.SemaphoreType.DMA
    anyspace = pl.BlockSpec(memory_space=pl.ANY)
    smem = pl.BlockSpec(memory_space=pltpu.SMEM)
    return pl.pallas_call(
        ring_kernel,
        out_shape=(
            jax.ShapeDtypeStruct((UBD,) + block, jnp.bfloat16),
            jax.ShapeDtypeStruct((2, CHIPS, 2) + block, jnp.bfloat16),
        ),
        in_specs=[smem] * 4 + [anyspace] * 3,
        out_specs=(anyspace, anyspace),
        scratch_shapes=[
            pltpu.VMEM((CHIPS, UBD) + block, jnp.bfloat16),
            pltpu.VMEM((CHIPS, 2 * UBD, UB), jnp.int32),
            pltpu.VMEM((CHIPS, UBD) + block, jnp.bfloat16),
            pltpu.VMEM((2 * BLK_DEV,) + block, jnp.bfloat16),
            pltpu.VMEM((UBD,) + block, jnp.bfloat16),
            pltpu.VMEM((DEPTH, SLOTS) + block, jnp.bfloat16),
            pltpu.VMEM((DEPTH, 8, UB), jnp.int32),
            pltpu.VMEM((DEPTH, SLOTS, BLK, UB), jnp.float32),
            pltpu.VMEM((DEPTH, 3, BLK, UB), jnp.float32),
            pltpu.VMEM((DEPTH, SLOTS, BLK, UB), jnp.bfloat16),
            pltpu.VMEM((3, SLOTS) + block, jnp.float32),
            pltpu.VMEM((DEPTH, SLOTS) + block, jnp.bfloat16),
            dma((3,)), dma((2,)),
            dma((CHIPS, HALVES)), dma((CHIPS, HALVES)), dma((CHIPS,)), dma((CHIPS,)),
            dma((CHIPS, HALVES)), dma((CHIPS, HALVES)),
            dma((DEPTH, 3)), dma((DEPTH, 3)), dma((DEPTH, 3)), dma((DEPTH, 3)),
            dma((DEPTH,)), dma((CHIPS,)), dma((DEPTH,)), dma,
        ],
        compiler_params=pltpu.CompilerParams(
            collective_id=0, has_side_effects=True, vmem_limit_bytes=60 * 1024 * 1024),
        name="ring",
    )(ku, lb, bid, scale, utter, labs, intents)


CHUNK = 16


def gather_kernel(lb_ref, con_ref, out_ref, acc):
    i = pl.program_id(0)

    @pl.when(i == 0)
    def _():
        acc[...] = jnp.zeros_like(acc)

    for k in range(CHUNK):
        b = lb_ref[i * CHUNK + k]
        acc[b] = acc[b] + con_ref[k].astype(jnp.float32)

    @pl.when(i == pl.num_programs(0) - 1)
    def _():
        out_ref[...] = acc[...].astype(out_ref.dtype)


def gather(lb, con):
    count, width = con.shape[0], con.shape[2]
    return pl.pallas_call(
        gather_kernel,
        grid_spec=pltpu.PrefetchScalarGridSpec(
            num_scalar_prefetch=1,
            grid=(count // CHUNK,),
            in_specs=[pl.BlockSpec((CHUNK, BLK, width), lambda i, t: (i, 0, 0))],
            out_specs=pl.BlockSpec((BLK_DEV, BLK, width), lambda i, t: (0, 0, 0)),
            scratch_shapes=[pltpu.VMEM((BLK_DEV, BLK, width), jnp.float32)],
        ),
        out_shape=jax.ShapeDtypeStruct((BLK_DEV, BLK, width), jnp.bfloat16),
        compiler_params=pltpu.CompilerParams(vmem_limit_bytes=40 * 1024 * 1024),
        name="sum_blocks",
    )(lb, con)


def plan(req_blocks, req_count, block_home):
    z = lax.axis_index("dp")
    cl = lax.axis_index("cls")
    chip = (cl // 2) * NZ + z
    base = (z * 2 * NY + (cl // 2) * 2) * BLK_DEV
    order = lax.dynamic_index_in_dim(jnp.asarray(ORDER), chip, 0, keepdims=False).reshape(2 * CHIPS)
    entries = UBD * MOST
    req = req_blocks.reshape(2 * CHIPS, entries)[order]
    count = req_count.reshape(2 * CHIPS, UBD)[order]
    place = jnp.arange(2 * BLK_DEV)
    ids = jnp.sum(
        jnp.where(block_home[None, :] == base + place[:, None], jnp.arange(block_home.shape[0])[None, :], 0), axis=1)
    local = jnp.sum(jnp.where(req[:, :, None] == ids[None, None, :], place[None, None, :] + 1, 0), axis=2) - 1
    at = jnp.arange(entries)[None, None, :]
    owner = jnp.arange(2)[None, :, None]
    mine = (local[:, None, :] >= 0) & (local[:, None, :] // BLK_DEV == owner)
    first = jnp.min(jnp.where(mine, at, entries), axis=2)
    last = jnp.max(jnp.where(mine, at, -1), axis=2)
    entry = jnp.stack([first, last], axis=2)
    valid = jnp.stack([last >= 0, last > first], axis=2)
    hot = (at[..., None, :] == entry[..., None]) & valid[..., None]
    lb = jnp.sum(jnp.where(hot, local[:, None, None, :], 0), axis=3)
    bid = jnp.sum(jnp.where(hot, req[:, None, None, :], 0), axis=3)
    ku = jnp.where(valid, entry // MOST, 0)
    listed = jnp.sum(jnp.where(ku[..., None] == jnp.arange(UBD), count[:, None, None, :], 0), axis=3)
    scale = jnp.where(valid, GAMMA / listed.astype(jnp.float32), 0.0)
    return ku, lb, bid, scale


def shards(utter, intents, req_blocks, req_count, block_home, labels):
    core = lax.axis_index("cls") % 2
    width = intents.shape[1]
    ku, lb, bid, scale = plan(req_blocks, req_count, block_home)

    def row(t, c):
        return lax.dynamic_index_in_dim(t.reshape(2, CHIPS, SLOTS), c, 0, keepdims=False).reshape(CHIPS * SLOTS)

    labs = labels.reshape(UBD, UB, 2).transpose(2, 0, 1).reshape(2 * UBD, UB)
    grad_utter, con = ring(
        row(ku, core), row(lb, core), row(bid, core), row(scale, core),
        utter.reshape(UBD, UB, width), labs, intents.reshape(BLK_DEV, BLK, width))
    near = lax.dynamic_index_in_dim(lb.reshape(2, CHIPS, 2, 2), core, 2, keepdims=False).reshape(4 * CHIPS) % BLK_DEV
    grad_intents = gather(near, con.reshape(4 * CHIPS, BLK, width))
    return grad_utter.reshape(UBD * UB, width), grad_intents.reshape(BLK_DEV * BLK, width)


def solution(mesh):
    return jax.shard_map(
        shards,
        mesh=mesh,
        in_specs=(
            P(("dp", "cls"), "feat"),
            P(("dp", "cls"), "feat"),
            P(),
            P(),
            P(),
            P(("dp", "cls"), None),
        ),
        out_specs=(P(("dp", "cls"), "feat"), P(("dp", "cls"), "feat")),
        check_vma=False,
    )
```

time: 665 us -> 251 us (0.38)
  waiting for transfers between devices: 455 us -> 0 us
  Pallas kernels: 0 us -> 228 us
  local copies, waits for them, and re-layouts: 112 us -> 12.9 us
  matrix products: 28.2 us -> 0 us
  other arithmetic: 29.9 us -> 4.36 us
  starting transfers between devices: 22.3 us -> 0 us
  between operations: 14.3 us -> 0.84 us
    all_to_all x2 -> x0, waiting for transfers between devices: 359 us -> none  [the longest x1 183 us: shards(): lax.all_to_all(outgoing, ('dp', 'cls'), split_axis=0, concat_axis=0, tile...]
    pallas_call x0 -> x2, Pallas kernels: none -> 228 us  [the longest x1 223 us: ring(): pl.pallas_call(ring_kernel, out_shape=(jax.ShapeDtypeStruct((UBD,) + bloc...]
    psum x1 -> x0, waiting for transfers between devices: 95.6 us -> none  [shards(): summed_live = lax.psum(packed, 'feat')]
    gather x6 -> x3, local copies, waits for them, and re-layouts: 86.6 us -> 1.26 us  [the longest x2 0.66 us: plan(): count = req_count.reshape(2 * CHIPS, UBD)[order]]
    dot_general x4 -> x0, matrix products: 28.2 us -> none  [the longest x1 8.94 us: shards(): jnp.einsum('bud,bmcd->bmuc', row_blocks, list_blocks, preferred_element_t...]
    all_to_all x2 -> x0, starting transfers between devices: 22 us -> none  [the longest x1 11.5 us: shards(): lax.all_to_all(outgoing, ('dp', 'cls'), split_axis=0, concat_axis=0, tile...]
    select_n x8 -> x5, other arithmetic: 14.5 us -> 0.07 us  [the longest x2 0.04 us: plan(): ku = jnp.where(valid, entry // MOST, 0)]
    unnamed x11 -> x7, local copies, waits for them, and re-layouts: 14.4 us -> 6.36 us
  transfers between devices with their start and end apart: 3 -> 0, of which waited for: 3 -> 0; matrix products, arithmetic and copies ran while one was open for 2% -> 0% of each run, Pallas kernels for 0% -> 0%
where the time goes in v1:
time: 251 us; the launch traced here: 247 us
  Pallas kernels  228 us (91%)
  local copies, waits for them, and re-layouts  12.9 us (5%)
  other arithmetic  4.36 us (2%)
    pallas_call x1, Pallas kernels, ring(): pl.pallas_call(ring_kernel, out_shape=(jax.ShapeDtypeStruct((UBD,) + bloc...  223 us
    unnamed x7, local copies, waits for them, and re-layouts  6.36 us
    pallas_call x1, Pallas kernels, gather(): pl.pallas_call(gather_kernel, grid_spec=pltpu.PrefetchScalarGridSpec(num_...  5.29 us

profile of v1, /device:TPU:64, one launch (start us, length us, event | category | flops | bytes accessed | tf_op | source)
XLA Modules:
  0.0 246.6 jit_solution(9281669450873781232)
XLA Ops:
  0.7 1.1 select_reduce_fusion.1
  1.8 0.7 constant_dynamic-slice_fusion.7
  2.6 1.3 copy.40
  3.9 0.8 reshape.270
  4.7 0.6 gather_fusion.1
  5.3 0.9 copy.25
  6.2 0.1 reshape.263
  6.4 0.6 gather_fusion
  7.0 2.6 %select_reduce_fusion = s32[64,128]{1,0:T(8,128)S(1)} fusion(s32[128]{0:T(128)S(1)} %iota_add_fusion, s32[128]{0:T(128)S(1)} %select_reduce_fusion.1, s32[64,128]{1,0:T(8,128)S(1)} %gather_fusion), kind=kLoop, calls=%fused_computation.2 | loop fusion | flops 3137536 | bytes 66560 | tf_op jit(solution)/shard_map/reduce_sum | solution.py:402
  9.6 0.1 select_reduce_fusion.5
  9.8 0.3 select_reduce_fusion.2
  10.7 0.1 copy.28
  10.8 0.6 reshape.265.ku_ref
  11.4 0.1 copy.31
  11.5 0.6 reshape.267.lb_ref
  12.2 0.6 reshape.271.scale_ref
  12.8 0.1 copy.32
  12.9 0.7 reshape.269.bid_ref
  13.6 0.1 copy.37
  13.7 0.1 reshape.278
  13.9 223.2 %ring.1 = (bf16[8,128,256]{2,1,0:T(8,128)(2,1)}, bf16[2,32,2,128,256]{4,3,2,1,0:T(8,128)(2,1)}) custom-call(s32[128]{0:T(128)} %reshape.265.ku_ref, s32[128]{0:T(128)} %reshape.267.lb_ref, s32[128]{0:T(128)} %reshape.269.bid_ref, f32[128]{0:T(128)} %reshape.271.scale_ref, bf16[8,128,256]{2,1,0:T(8,128)(2,1)} %bitcast.41, s32[16,128]{1,0:T(8,128)} %bitcast.44, ...), custom_call_target="tpu_custom_call" | custom-call | tf_op jit(solution)/shard_map/ring/pallas_call | solution.py:321
  237.1 3.4 %copy-done = bf16[2,32,2,128,256]{4,3,2,1,0:T(8,128)(2,1)S(1)} copy-done((bf16[2,32,2,128,256]{4,3,2,1,0:T(8,128)(2,1)S(1)}, bf16[2,32,2,128,256]{4,3,2,1,0:T(8,128)(2,1)}, u32[]{:S(2)}) %copy-start) | copy-done | bytes 8388632
  240.5 5.3 %sum_blocks.1 = bf16[64,128,256]{2,1,0:T(8,128)(2,1)} custom-call(s32[128]{0:T(128)S(1)} %and_select_fusion.2.lb_ref, bf16[128,128,256]{2,1,0:T(8,128)(2,1)S(1)} %bitcast.38), custom_call_target="tpu_custom_call" | custom-call | tf_op jit(solution)/shard_map/sum_blocks/pallas_call | solution.py:375
  245.8 0.8 copy.42
  (32 shorter events, 0.9 us)
Async XLA Ops:
  237.1 3.4 %copy-start = (bf16[2,32,2,128,256]{4,3,2,1,0:T(8,128)(2,1)S(1)}, bf16[2,32,2,128,256]{4,3,2,1,0:T(8,128)(2,1)}, u32[]{:S(2)}) copy-start(bf16[2,32,2,128,256]{4,3,2,1,0:T(8,128)(2,1)} %get-tuple-element.5) | copy-start | bytes 25165828
  240.5 5.3 %copy-start.1 = (bf16[8,128,256]{2,1,0:T(8,128)(2,1)S(1)}, bf16[8,128,256]{2,1,0:T(8,128)(2,1)}, u32[]{:S(2)}) copy-start(bf16[8,128,256]{2,1,0:T(8,128)(2,1)} %get-tuple-element.4) | copy-start | bytes 1572868

commit v2 on v0

v2 whole, which is shorter than its diff:
```python
import jax
import jax.numpy as jnp
import numpy as np
from jax import lax
from jax.experimental import pallas as pl
from jax.experimental.pallas import tpu as pltpu
from jax.sharding import PartitionSpec as P

BLK = 128
BLK_DEV = 64
UB = 128
UBD = 8
MOST = 16
GAMMA = 4.0
MARGIN = 0.25

NY, NZ = 4, 8
CHIPS = NY * NZ
SLOTS = 4
DEPTH = 8
CON_DEPTH = 4
LAG_SLOPE = 2
LAG_GRAD = 4
PARTS = 2
PART = UBD // PARTS
ROWS = 32
MESH = pl.DeviceIdType.MESH

NODES = (
    (0, 0, -1, -1, 1),
    (1, 0, 0, 2, 1),
    (0, 1, 0, 0, 1),
    (0, 7, 0, 1, 0),
    (2, 0, 1, 2, 1),
    (0, 2, 2, 0, 1),
    (3, 1, 2, 3, 0),
    (3, 0, 4, 2, 0),
    (2, 7, 4, 1, 1),
    (2, 1, 4, 0, 0),
    (1, 2, 5, 2, 1),
    (0, 3, 5, 0, 1),
    (3, 2, 5, 3, 0),
    (1, 7, 8, 3, 0),
    (2, 6, 8, 1, 1),
    (3, 3, 11, 3, 1),
    (1, 1, 10, 1, 0),
    (0, 4, 11, 0, 1),
    (1, 6, 14, 3, 0),
    (3, 6, 14, 2, 0),
    (2, 3, 15, 3, 1),
    (2, 5, 14, 1, 0),
    (0, 5, 17, 0, 1),
    (2, 2, 20, 1, 0),
    (2, 4, 20, 0, 0),
    (3, 5, 22, 3, 0),
    (1, 5, 22, 2, 0),
    (0, 6, 22, 0, 0),
    (3, 4, 15, 0, 0),
    (1, 4, 17, 2, 0),
    (1, 3, 20, 3, 0),
    (3, 7, 8, 2, 0),
)
TASKS = (
    (("A", 0, 0), ("A", 0, 1),),
    (("A", 1, 0), ("A", 2, 0), ("A", 1, 1), ("A", 2, 1),),
    (),
    (("A", 4, 0),),
    (("A", 4, 1),),
    (("A", 5, 0), ("A", 5, 1),),
    (),
    (("A", 8, 0),),
    (("A", 8, 1), ("A", 10, 0),),
    (("A", 10, 1),),
    (("A", 11, 0),),
    (("A", 11, 1),),
    (("A", 14, 0),),
    (("A", 15, 0),),
    (("A", 14, 1),),
    (("A", 17, 0), ("A", 15, 1),),
    (),
    (("A", 17, 1), ("A", 20, 0),),
    (),
    (),
    (("A", 22, 0), ("A", 20, 1),),
    (),
    (("A", 22, 1),),
    (),
    (),
    (("R", 10, 0), ("R", 10, 1),),
    (),
    (),
    (("R", 14, 0), ("R", 14, 1),),
    (),
    (),
    (),
    (),
    (),
    (("R", 22, 0), ("R", 22, 1),),
    (),
)
LAST = (("R", 17, 0), ("R", 20, 0), ("R", 20, 1), ("R", 17, 1), ("R", 8, 0), ("R", 8, 1), ("R", 15, 0), ("R", 15, 1), ("R", 4, 0), ("R", 11, 0), ("R", 4, 1), ("R", 11, 1), ("R", 5, 0), ("R", 1, 0), ("R", 5, 1), ("R", 1, 1), ("R", 2, 0), ("R", 2, 1), ("R", 0, 0), ("R", 0, 1),)

DIRS = ((0, 1), (0, -1), (1, 0), (-1, 0))
INNER = [k for k in range(CHIPS) if NODES[k][4]]
OUTER = [k for k in range(CHIPS) if not NODES[k][4]]
SPOT = {k: i for i, k in enumerate(INNER)}
SPOT.update({k: i for i, k in enumerate(OUTER)})
KIDS = {k: [c for c in range(CHIPS) if NODES[c][2] == k] for k in range(CHIPS)}


def _sources():
    rows = np.zeros((CHIPS, 2, 3 * CHIPS), np.int32)
    goal = np.zeros((CHIPS, 2, 3 * CHIPS), np.int32)
    for y in range(NY):
        for z in range(NZ):
            for core in range(2):
                out, aim = [], []
                for c in range(2):
                    sign = 1 - 2 * c
                    for dy, dz, *_ in NODES:
                        out.append((z - sign * dz) % NZ * 2 * NY + (y - sign * dy) % NY * 2 + c)
                        aim.append(z * NY + y)
                sign = 1 - 2 * core
                for dy, dz, parent, way, _ in NODES:
                    step = DIRS[way] if parent >= 0 else (0, 0)
                    py, pz = y + sign * step[0], z + sign * step[1]
                    out.append((pz - sign * dz) % NZ * 2 * NY + (py - sign * dy) % NY * 2 + core)
                    aim.append(pz % NZ * NY + py % NY)
                rows[y * NZ + z, core], goal[y * NZ + z, core] = out, aim
    return rows, goal


SOURCE, GOAL = _sources()


def tree_kernel(
    ku_ref, lb_ref, bid_ref, scale_ref, kid_ref, utter_ref, lab_ref, intents_ref,
    gu_ref, con_ref,
    ag, outer, stage, aglab, rsin, rep, w, ucur, usel, labsel, part, recv, gs, gown, gbuf, cst,
    sem_in, sem_w, ag_send, ag_recv, out_send, out_recv, lab_send, lab_recv, rs_send, rs_recv, rep_send, rep_recv,
    part_send, part_recv, gs_send, gs_recv, con_send, con_recv, con_loc, sem_out,
):
    z = lax.axis_index("dp")
    cl = lax.axis_index("cls")
    x = lax.axis_index("feat")
    y = cl // 2
    core = cl % 2
    sign = 1 - 2 * core

    def toward(way, back=False):
        dy, dz = DIRS[way]
        flip = -sign if back else sign
        return ((z + NZ + flip * dz) % NZ, (y + NY + flip * dy) % NY * 2 + core, x)

    other = (z, y * 2 + (1 - core), x)

    def peer(o):
        return (z, cl, (x + o) % 4)

    def remote(src, dst, send, recv_sem, device):
        return pltpu.make_async_remote_copy(
            src_ref=src, dst_ref=dst, send_sem=send, recv_sem=recv_sem, device_id=device, device_id_type=MESH)

    def ag_copy(k, h):
        piece = pl.ds(h * PART, PART)
        return remote(ag.at[SPOT[NODES[k][2]], piece], ag.at[SPOT[k], piece],
                      ag_send.at[SPOT[k], h], ag_recv.at[SPOT[k], h], toward(NODES[k][3]))

    def out_copy(k):
        return remote(stage.at[SPOT[k]], outer.at[SPOT[k]], out_send.at[SPOT[k]], out_recv.at[SPOT[k]], toward(NODES[k][3]))

    def lab_copy(k):
        return remote(aglab.at[NODES[k][2]], aglab.at[k], lab_send.at[k], lab_recv.at[k], toward(NODES[k][3]))

    def rs_copy(k, h):
        piece = pl.ds(h * PART, PART)
        return remote(ag.at[SPOT[k], piece], rsin.at[SPOT[k], piece],
                      rs_send.at[SPOT[k], h], rs_recv.at[SPOT[k], h], toward(NODES[k][3], True))

    def rep_copy(k):
        return remote(outer.at[SPOT[k]], rep.at[SPOT[k]], rep_send.at[SPOT[k]], rep_recv.at[SPOT[k]], toward(NODES[k][3], True))

    def part_copy(n, o):
        return remote(part.at[n % DEPTH, (x + o) % 4], recv.at[n % DEPTH, o - 1],
                      part_send.at[n % DEPTH, o - 1], part_recv.at[n % DEPTH, o - 1], peer(o))

    def gs_copy(m, o):
        return remote(gs.at[m % DEPTH, x], gs.at[m % DEPTH, x],
                      gs_send.at[m % DEPTH, o - 1], gs_recv.at[m % DEPTH, o - 1], peer(o))

    def gs_wait(m, o):
        place = gs.at[m % DEPTH, (x + 4 - o) % 4]
        remote(place, place, gs_send.at[m % DEPTH, o - 1], gs_recv.at[m % DEPTH, o - 1], peer(o)).wait_recv()

    def con_far(m):
        return remote(cst.at[m % CON_DEPTH, pl.ds(2 * (1 - core), 2)], con_ref.at[core, m],
                      con_send.at[m % CON_DEPTH], con_recv.at[m], other)

    def con_far_wait(m):
        remote(cst.at[m % CON_DEPTH, pl.ds(2 * (1 - core), 2)], con_ref.at[1 - core, m],
               con_send.at[m % CON_DEPTH], con_recv.at[m], other).wait_recv()

    def con_near(m):
        return pltpu.make_async_copy(
            cst.at[m % CON_DEPTH, pl.ds(2 * core, 2)], con_ref.at[core, m], con_loc.at[m % CON_DEPTH])

    def out_dma(h):
        piece = pl.ds(h * PART, PART)
        return pltpu.make_async_copy(ag.at[0, piece], gu_ref.at[piece], sem_out.at[h])

    own_u = pltpu.make_async_copy(utter_ref, ag.at[0], sem_in.at[0])
    own_l = pltpu.make_async_copy(lab_ref, aglab.at[0], sem_in.at[1])
    own_w = pltpu.make_async_copy(intents_ref, w.at[pl.ds(core * BLK_DEV, BLK_DEV)], sem_in.at[2])
    far_w = remote(intents_ref, w.at[pl.ds(core * BLK_DEV, BLK_DEV)], sem_w.at[0], sem_w.at[1], other)
    far_w_in = remote(intents_ref, w.at[pl.ds((1 - core) * BLK_DEV, BLK_DEV)], sem_w.at[0], sem_w.at[1], other)
    own_u.start()
    own_l.start()
    own_w.start()

    barrier = pltpu.get_barrier_semaphore()
    for device in [toward(way) for way in range(4)] + [other, peer(1), peer(2), peer(3)]:
        pl.semaphore_signal(barrier, inc=1, device_id=device, device_id_type=MESH)
    pl.semaphore_wait(barrier, 8)
    own_u.wait()
    own_l.wait()
    far_w.start()

    def pass_on(k, h):
        if k > 0:
            ag_copy(k, h).wait_recv()
            if h == 0:
                lab_copy(k).wait_recv()
        for c in KIDS[k]:
            if NODES[c][4]:
                ag_copy(c, h).start()
                if h == 0:
                    lab_copy(c).start()

    def pick(k):
        d = k % DEPTH
        if NODES[k][4]:
            for j in range(UBD):
                ucur[j] = ag[SPOT[k], j]
            for c in KIDS[k]:
                if not NODES[c][4]:
                    for s in range(SLOTS):
                        stage[SPOT[c], s] = ucur[kid_ref[c * SLOTS + s]]
                    out_copy(c).start()
                    lab_copy(c).start()
            for s in range(SLOTS):
                usel[d, s] = ucur[ku_ref[k * SLOTS + s]]
        else:
            out_copy(k).wait_recv()
            lab_copy(k).wait_recv()
            for s in range(SLOTS):
                usel[d, s] = outer[SPOT[k], s]

    def scores(n):
        d = n % DEPTH

        @pl.when(n >= DEPTH)
        def _():
            for o in range(1, 4):
                part_copy(n, o).wait_send()

        mine = ku_ref[n * SLOTS + x]
        rows = lax.broadcasted_iota(jnp.int32, (UBD, UB), 0)
        for k in range(2):
            labs = aglab[n, k * UBD:(k + 1) * UBD]
            labsel[d, k:k + 1] = jnp.sum(jnp.where(rows == mine, labs, 0), axis=0, keepdims=True)
        for s in range(SLOTS):
            part[d, s] = lax.dot_general(
                w[lb_ref[n * SLOTS + s]], usel[d, s], (((1,), (1,)), ((), ())),
                preferred_element_type=jnp.float32).astype(part.dtype)
        for o in range(1, 4):
            part_copy(n, o).start()

    def slopes(m):
        d = m % DEPTH

        @pl.when(m >= DEPTH)
        def _():
            for o in range(1, 4):
                gs_copy(m, o).wait_send()

        total = part[d, x].astype(jnp.float32)
        for o in range(1, 4):
            part_copy(m, o).wait_recv()
            total = total + recv[d, o - 1].astype(jnp.float32)
        logits = GAMMA * total
        ids = lax.broadcasted_iota(jnp.int32, (BLK, UB), 0) + bid_ref[m * SLOTS + x] * BLK
        hit = (ids == labsel[d, 0:1]) | (ids == labsel[d, 1:2])
        slope = jax.nn.sigmoid(jnp.where(hit, MARGIN - logits, logits + MARGIN))
        slope = jnp.where(hit, -slope, slope) * scale_ref[m * SLOTS + x]
        gs[d, x] = slope.astype(jnp.bfloat16)
        for o in range(1, 4):
            gs_copy(m, o).start()

    def grads(m):
        d = m % DEPTH
        e = m % CON_DEPTH

        @pl.when(m >= CON_DEPTH)
        def _():
            con_far(m).wait_send()
            con_near(m).wait()

        for o in range(1, 4):
            gs_wait(m, o)
        for s in range(SLOTS):
            slope = gs[d, s]
            cst[e, s] = jnp.dot(slope, usel[d, s], preferred_element_type=jnp.float32).astype(jnp.bfloat16)
            gown[s] = lax.dot_general(
                slope, w[lb_ref[m * SLOTS + s]], (((0,), (0,)), ((), ())),
                preferred_element_type=jnp.float32)
        con_far(m).start()
        con_near(m).start()

    def keep(k):
        if NODES[k][4]:
            for s in range(SLOTS):
                gbuf[SPOT[k], s] = gown[s]
        else:
            for s in range(SLOTS):
                outer[SPOT[k], s] = gown[s].astype(jnp.bfloat16)
            rep_copy(k).start()

    def fold(k, h):
        inner = [c for c in KIDS[k] if NODES[c][4]]
        outer_kids = [c for c in KIDS[k] if not NODES[c][4]]
        for c in inner:
            rs_copy(c, h).wait_recv()
            ag_copy(c, h).wait_send()
        if h == 0:
            for c in outer_kids:
                rep_copy(c).wait_recv()
        tiles = UB // ROWS

        def tile(i, carry):
            j = h * PART + i // tiles
            rows = pl.ds(pl.multiple_of(i % tiles * ROWS, ROWS), ROWS)
            total = jnp.zeros((ROWS, ag.shape[3]), jnp.float32)
            for s in range(SLOTS):
                total = total + gbuf[SPOT[k], s, rows] * (ku_ref[k * SLOTS + s] == j).astype(jnp.float32)
            for c in outer_kids:
                for s in range(SLOTS):
                    share = (kid_ref[c * SLOTS + s] == j).astype(jnp.float32)
                    total = total + rep[SPOT[c], s, rows].astype(jnp.float32) * share
            for c in inner:
                total = total + rsin[SPOT[c], j, rows].astype(jnp.float32)
            ag[SPOT[k], j, rows] = total.astype(jnp.bfloat16)
            return carry

        lax.fori_loop(0, PART * tiles, tile, 0)
        if k == 0:
            out_dma(h).start()
        else:
            rs_copy(k, h).start()

    def do(tasks):
        for kind, k, h in tasks:
            if kind == "A":
                pass_on(k, h)
            else:
                fold(k, h)

    def step(n, carry):
        for k in range(len(TASKS)):
            if k < CHIPS or TASKS[k]:
                @pl.when(n == k)
                def _():
                    do(TASKS[k])
                    if k < CHIPS:
                        pick(k)
                    if k == 0:
                        own_w.wait()
                        far_w_in.wait_recv()

        @pl.when(n < CHIPS)
        def _():
            scores(n)

        @pl.when((n >= LAG_SLOPE) & (n < CHIPS + LAG_SLOPE))
        def _():
            slopes(n - LAG_SLOPE)

        @pl.when(n >= LAG_GRAD)
        def _():
            grads(n - LAG_GRAD)

        for k in range(CHIPS):
            @pl.when(n == k + LAG_GRAD)
            def _():
                keep(k)
        return carry

    lax.fori_loop(0, CHIPS + LAG_GRAD, step, 0)
    do(LAST)

    for k in range(1, CHIPS):
        lab_copy(k).wait_send()
        if NODES[k][4]:
            for h in range(PARTS):
                rs_copy(k, h).wait_send()
        else:
            out_copy(k).wait_send()
            rep_copy(k).wait_send()

    def drain(n, carry):
        con_far_wait(n)
        return carry

    lax.fori_loop(0, CHIPS, drain, 0)
    for n in range(CHIPS - DEPTH, CHIPS):
        for o in range(1, 4):
            part_copy(n, o).wait_send()
            gs_copy(n, o).wait_send()
    for n in range(CHIPS - CON_DEPTH, CHIPS):
        con_far(n).wait_send()
        con_near(n).wait()
    far_w.wait_send()
    for h in range(PARTS):
        out_dma(h).wait()


def tree(ku, lb, bid, scale, kid, utter, labs, intents):
    width = intents.shape[2]
    block = (UB, width)
    dma = pltpu.SemaphoreType.DMA
    anyspace = pl.BlockSpec(memory_space=pl.ANY)
    smem = pl.BlockSpec(memory_space=pltpu.SMEM)
    ni, no = len(INNER), len(OUTER)
    bf16 = jnp.bfloat16
    return pl.pallas_call(
        tree_kernel,
        out_shape=(
            jax.ShapeDtypeStruct((UBD,) + block, bf16),
            jax.ShapeDtypeStruct((2, CHIPS, 2) + block, bf16),
        ),
        in_specs=[smem] * 5 + [anyspace] * 3,
        out_specs=(anyspace, anyspace),
        scratch_shapes=[
            pltpu.VMEM((ni, UBD) + block, bf16),
            pltpu.VMEM((no, SLOTS) + block, bf16),
            pltpu.VMEM((no, SLOTS) + block, bf16),
            pltpu.VMEM((CHIPS, 2 * UBD, UB), jnp.int32),
            pltpu.VMEM((ni, UBD) + block, bf16),
            pltpu.VMEM((no, SLOTS) + block, bf16),
            pltpu.VMEM((2 * BLK_DEV,) + block, bf16),
            pltpu.VMEM((UBD,) + block, bf16),
            pltpu.VMEM((DEPTH, SLOTS) + block, bf16),
            pltpu.VMEM((DEPTH, 8, UB), jnp.int32),
            pltpu.VMEM((DEPTH, SLOTS, BLK, UB), SCORE),
            pltpu.VMEM((DEPTH, 3, BLK, UB), SCORE),
            pltpu.VMEM((DEPTH, SLOTS, BLK, UB), bf16),
            pltpu.VMEM((SLOTS,) + block, jnp.float32),
            pltpu.VMEM((ni, SLOTS) + block, jnp.float32),
            pltpu.VMEM((CON_DEPTH, SLOTS) + block, bf16),
            dma((3,)), dma((2,)),
            dma((ni, PARTS)), dma((ni, PARTS)), dma((no,)), dma((no,)), dma((CHIPS,)), dma((CHIPS,)),
            dma((ni, PARTS)), dma((ni, PARTS)), dma((no,)), dma((no,)),
            dma((DEPTH, 3)), dma((DEPTH, 3)), dma((DEPTH, 3)), dma((DEPTH, 3)),
            dma((CON_DEPTH,)), dma((CHIPS,)), dma((CON_DEPTH,)), dma((PARTS,)),
        ],
        compiler_params=pltpu.CompilerParams(
            collective_id=0, has_side_effects=True, vmem_limit_bytes=60 * 1024 * 1024),
        name="tree",
    )(ku, lb, bid, scale, kid, utter, labs, intents)


SCORE = jnp.bfloat16
CHUNK = 16


def gather_kernel(lb_ref, con_ref, out_ref, con, acc, res, sem_in, sem_out):
    count = con.shape[0]

    def load(i):
        piece = pl.ds(i * CHUNK, CHUNK)
        return pltpu.make_async_copy(con_ref.at[piece], con.at[piece], sem_in.at[i])

    def store(i):
        piece = pl.ds(i * CHUNK, CHUNK)
        return pltpu.make_async_copy(res.at[piece], out_ref.at[piece], sem_out.at[i])

    for i in range(count // CHUNK):
        load(i).start()
    acc[...] = jnp.zeros_like(acc)
    for i in range(count // CHUNK):
        load(i).wait()

        def add(k, carry):
            b = lb_ref[i * CHUNK + k]
            acc[b] = acc[b] + con[i * CHUNK + k].astype(jnp.float32)
            return carry

        lax.fori_loop(0, CHUNK, add, 0)
    for i in range(BLK_DEV // CHUNK):
        piece = pl.ds(i * CHUNK, CHUNK)
        res[piece] = acc[piece].astype(res.dtype)
        store(i).start()
    for i in range(BLK_DEV // CHUNK):
        store(i).wait()


def gather(lb, con):
    count, width = con.shape[0], con.shape[2]
    dma = pltpu.SemaphoreType.DMA
    return pl.pallas_call(
        gather_kernel,
        in_specs=[pl.BlockSpec(memory_space=pltpu.SMEM), pl.BlockSpec(memory_space=pl.ANY)],
        out_specs=pl.BlockSpec(memory_space=pl.ANY),
        scratch_shapes=[
            pltpu.VMEM((count, BLK, width), jnp.bfloat16),
            pltpu.VMEM((BLK_DEV, BLK, width), jnp.float32),
            pltpu.VMEM((BLK_DEV, BLK, width), jnp.bfloat16),
            dma((count // CHUNK,)), dma((BLK_DEV // CHUNK,)),
        ],
        out_shape=jax.ShapeDtypeStruct((BLK_DEV, BLK, width), jnp.bfloat16),
        compiler_params=pltpu.CompilerParams(vmem_limit_bytes=60 * 1024 * 1024),
        name="sum_blocks",
    )(lb, con)


def plan(req_blocks, req_count, block_home):
    z = lax.axis_index("dp")
    cl = lax.axis_index("cls")
    chip, core = (cl // 2) * NZ + z, cl % 2
    rows = lax.dynamic_slice(jnp.asarray(SOURCE), (chip, core, 0), (1, 1, 3 * CHIPS)).reshape(3 * CHIPS)
    goal = lax.dynamic_slice(jnp.asarray(GOAL), (chip, core, 0), (1, 1, 3 * CHIPS)).reshape(3 * CHIPS)
    entries = UBD * MOST
    wide = 64
    req = req_blocks.reshape(2 * CHIPS * entries)
    spread = (jnp.arange(wide)[:, None] == (req // wide)[None, :]).astype(jnp.bfloat16)
    table = block_home.reshape(wide, wide).T
    halves = jnp.concatenate([table // wide, table % wide], axis=0).astype(jnp.bfloat16)
    found = jnp.dot(halves, spread, preferred_element_type=jnp.float32).reshape(2, wide, -1)
    low = jnp.arange(wide)[:, None] == (req % wide)[None, :]
    found = jnp.sum(jnp.where(low[None], found, 0.0), axis=1).astype(jnp.int32)
    home = jnp.where(req >= 0, found[0] * wide + found[1], -1)
    req = req.reshape(2 * CHIPS, entries)[rows]
    home = home.reshape(2 * CHIPS, entries)[rows]
    count = req_count.reshape(2 * CHIPS, UBD)[rows]
    at = jnp.arange(entries)[None, None, :]
    side = goal[:, None] * 2 + jnp.arange(2)[None, :]
    mine = (home[:, None, :] >= 0) & (home[:, None, :] // BLK_DEV == side[:, :, None])
    first = jnp.min(jnp.where(mine, at, entries), axis=2)
    last = jnp.max(jnp.where(mine, at, -1), axis=2)
    entry = jnp.stack([first, last], axis=2)
    valid = jnp.stack([last >= 0, last > first], axis=2)
    hot = (at[..., None, :] == entry[..., None]) & valid[..., None]
    lb = jnp.sum(jnp.where(hot, home[:, None, None, :] % (2 * BLK_DEV), 0), axis=3)
    bid = jnp.sum(jnp.where(hot, req[:, None, None, :], 0), axis=3)
    ku = jnp.where(valid, entry // MOST, 0)
    listed = jnp.sum(jnp.where(ku[..., None] == jnp.arange(UBD), count[:, None, None, :], 0), axis=3)
    scale = jnp.where(valid, GAMMA / listed.astype(jnp.float32), 0.0)
    return ku, lb, bid, scale


def shards(utter, intents, req_blocks, req_count, block_home, labels):
    core = lax.axis_index("cls") % 2
    width = intents.shape[1]
    ku, lb, bid, scale = plan(req_blocks, req_count, block_home)

    def row(t, c):
        return lax.dynamic_slice_in_dim(t.reshape(3 * CHIPS * SLOTS), c * CHIPS * SLOTS, CHIPS * SLOTS)

    labs = labels.reshape(UBD, UB, 2).transpose(2, 0, 1).reshape(2 * UBD, UB)
    grad_utter, con = tree(
        row(ku, core), row(lb, core), row(bid, core), row(scale, core), row(ku, 2),
        utter.reshape(UBD, UB, width), labs, intents.reshape(BLK_DEV, BLK, width))
    near = lax.dynamic_index_in_dim(
        lb[:2 * CHIPS].reshape(2 * CHIPS, 2, 2), core, 1, keepdims=False).reshape(4 * CHIPS) % BLK_DEV
    grad_intents = gather(near, con.reshape(4 * CHIPS, BLK, width))
    return grad_utter.reshape(UBD * UB, width), grad_intents.reshape(BLK_DEV * BLK, width)


def solution(mesh):
    return jax.shard_map(
        shards,
        mesh=mesh,
        in_specs=(
            P(("dp", "cls"), "feat"),
            P(("dp", "cls"), "feat"),
            P(),
            P(),
            P(),
            P(("dp", "cls"), None),
        ),
        out_specs=(P(("dp", "cls"), "feat"), P(("dp", "cls"), "feat")),
        check_vma=False,
    )
```

time: 665 us -> 190 us (0.29)
  waiting for transfers between devices: 455 us -> 0 us
  Pallas kernels: 0 us -> 171 us
  local copies, waits for them, and re-layouts: 112 us -> 11.8 us
  matrix products: 28.2 us -> 1.33 us
  other arithmetic: 29.9 us -> 3.08 us
  starting transfers between devices: 22.3 us -> 0 us
  between operations: 14.3 us -> 0.9 us
    all_to_all x2 -> x0, waiting for transfers between devices: 359 us -> none  [the longest x1 183 us: shards(): lax.all_to_all(outgoing, ('dp', 'cls'), split_axis=0, concat_axis=0, tile...]
    pallas_call x0 -> x2, Pallas kernels: none -> 171 us  [the longest x1 165 us: tree(): pl.pallas_call(tree_kernel, out_shape=(jax.ShapeDtypeStruct((UBD,) + bloc...]
    psum x1 -> x0, waiting for transfers between devices: 95.6 us -> none  [shards(): summed_live = lax.psum(packed, 'feat')]
    gather x6 -> x4, local copies, waits for them, and re-layouts: 86.6 us -> 1.92 us  [the longest x2 0.67 us: plan(): count = req_count.reshape(2 * CHIPS, UBD)[rows]]
    dot_general x4 -> x1, matrix products: 28.2 us -> 1.33 us  [plan(): jnp.dot(halves, spread, preferred_element_type=jnp.float32)]
    all_to_all x2 -> x0, starting transfers between devices: 22 us -> none  [the longest x1 11.5 us: shards(): lax.all_to_all(outgoing, ('dp', 'cls'), split_axis=0, concat_axis=0, tile...]
    select_n x8, other arithmetic: 14.5 us -> 1.37 us  [the longest x1 0.69 us: plan(): home = home.reshape(2 * CHIPS, entries)[rows]]
    unnamed x11 -> x5, local copies, waits for them, and re-layouts: 14.4 us -> 2.98 us
  transfers between devices with their start and end apart: 3 -> 0, of which waited for: 3 -> 0; matrix products, arithmetic and copies ran while one was open for 2% -> 0% of each run, Pallas kernels for 0% -> 0%
where the time goes in v2:
time: 190 us; the launch traced here: 188 us
  Pallas kernels  171 us (90%)
  local copies, waits for them, and re-layouts  11.8 us (6%)
  other arithmetic  3.08 us (2%)
    pallas_call x1, Pallas kernels, tree(): pl.pallas_call(tree_kernel, out_shape=(jax.ShapeDtypeStruct((UBD,) + bloc...  165 us
    pallas_call x1, Pallas kernels, gather(): pl.pallas_call(gather_kernel, in_specs=[pl.BlockSpec(memory_space=pltpu.S...  6.65 us

profile of v2, /device:TPU:64, one launch (start us, length us, event | category | flops | bytes accessed | tf_op | source)
XLA Modules:
  0.0 188.3 jit_solution(16961176926378686276)
XLA Ops:
  0.7 0.7 fusion.23
  1.4 0.7 fusion.21
  2.1 1.3 copy.35
  3.4 0.8 reshape.367
  4.1 0.6 gather_fusion.2
  4.8 0.8 reshape.362
  5.6 0.9 copy.20
  6.8 0.6 gather_fusion.1
  7.5 0.3 iota_compare_fusion.1
  7.7 1.3 select_reduce_fusion
  9.2 0.6 gather_fusion
  9.9 0.2 select_reduce_fusion.4
  10.3 0.4 select_reduce_fusion.1
  10.8 0.7 dynamic_slice.34.kid_ref
  11.7 0.6 and_select_fusion.1.lb_ref
  12.7 0.2 reshape.366
  12.9 0.6 dynamic_slice.31.bid_ref
  13.6 0.2 stack.17
  13.8 0.6 dynamic_slice.29.ku_ref
  14.7 0.6 dynamic_slice.32.scale_ref
  15.7 0.6 dynamic_slice.30.lb_ref
  16.2 164.6 %tree.1 = (bf16[8,128,256]{2,1,0:T(8,128)(2,1)}, bf16[2,32,2,128,256]{4,3,2,1,0:T(8,128)(2,1)}) custom-call(s32[128]{0:T(128)} %dynamic_slice.29.ku_ref, s32[128]{0:T(128)} %dynamic_slice.30.lb_ref, s32[128]{0:T(128)} %dynamic_slice.31.bid_ref, f32[128]{0:T(128)} %dynamic_slice.32.scale_ref, s32[128]{0:T(128)} %dynamic_slice.34.kid_ref, ...), custom_call_target="tpu_custom_call" | custom-call | tf_op jit(solution)/shard_map/tree/pallas_call | solution.py:434
  180.8 6.6 %sum_blocks.1 = bf16[64,128,256]{2,1,0:T(8,128)(2,1)} custom-call(s32[128]{0:T(128)} %and_select_fusion.1.lb_ref, bf16[128,128,256]{2,1,0:T(8,128)(2,1)} %bitcast.63), custom_call_target="tpu_custom_call" | custom-call | tf_op jit(solution)/shard_map/sum_blocks/pallas_call | solution.py:509
  187.5 0.8 copy.37
  (37 shorter events, 2.2 us)
Async XLA Ops:
  180.8 6.7 %copy-start = (bf16[8,128,256]{2,1,0:T(8,128)(2,1)S(1)}, bf16[8,128,256]{2,1,0:T(8,128)(2,1)}, u32[]{:S(2)}) copy-start(bf16[8,128,256]{2,1,0:T(8,128)(2,1)} %get-tuple-element.4) | copy-start | bytes 1572868

commit v3 on v2

--- a/solution.py
+++ b/solution.py
@@ -1,6 +1,5 @@
 import jax
 import jax.numpy as jnp
-import numpy as np
 from jax import lax
 from jax.experimental import pallas as pl
 from jax.experimental.pallas import tpu as pltpu
@@ -30,75 +29,75 @@
     (0, 0, -1, -1, 1),
     (1, 0, 0, 2, 1),
     (0, 1, 0, 0, 1),
-    (0, 7, 0, 1, 0),
+    (0, 7, 0, 1, 1),
     (2, 0, 1, 2, 1),
+    (3, 1, 2, 3, 0),
     (0, 2, 2, 0, 1),
-    (3, 1, 2, 3, 0),
-    (3, 0, 4, 2, 0),
+    (1, 1, 2, 2, 0),
+    (1, 7, 3, 2, 0),
     (2, 7, 4, 1, 1),
+    (0, 6, 3, 1, 0),
+    (3, 2, 6, 3, 0),
+    (0, 3, 6, 0, 1),
+    (3, 7, 3, 3, 0),
+    (2, 6, 9, 1, 1),
+    (1, 3, 12, 2, 1),
     (2, 1, 4, 0, 0),
-    (1, 2, 5, 2, 1),
-    (0, 3, 5, 0, 1),
-    (3, 2, 5, 3, 0),
-    (1, 7, 8, 3, 0),
-    (2, 6, 8, 1, 1),
-    (3, 3, 11, 3, 1),
-    (1, 1, 10, 1, 0),
-    (0, 4, 11, 0, 1),
+    (0, 4, 12, 0, 1),
+    (2, 5, 14, 1, 0),
     (1, 6, 14, 3, 0),
     (3, 6, 14, 2, 0),
-    (2, 3, 15, 3, 1),
-    (2, 5, 14, 1, 0),
+    (2, 3, 15, 2, 1),
+    (1, 2, 15, 1, 0),
+    (3, 4, 17, 3, 0),
+    (2, 4, 21, 0, 0),
     (0, 5, 17, 0, 1),
-    (2, 2, 20, 1, 0),
-    (2, 4, 20, 0, 0),
-    (3, 5, 22, 3, 0),
-    (1, 5, 22, 2, 0),
-    (0, 6, 22, 0, 0),
-    (3, 4, 15, 0, 0),
-    (1, 4, 17, 2, 0),
-    (1, 3, 20, 3, 0),
-    (3, 7, 8, 2, 0),
+    (2, 2, 21, 1, 0),
+    (3, 3, 21, 2, 0),
+    (1, 5, 25, 2, 0),
+    (3, 5, 25, 3, 0),
+    (1, 4, 15, 0, 0),
+    (3, 0, 4, 2, 0),
 )
 TASKS = (
     (("A", 0, 0), ("A", 0, 1),),
-    (("A", 1, 0), ("A", 2, 0), ("A", 1, 1), ("A", 2, 1),),
-    (),
-    (("A", 4, 0),),
+    (("A", 2, 0), ("A", 1, 0), ("A", 3, 0), ("A", 1, 1),),
+    (("A", 2, 1),),
+    (("A", 4, 0), ("A", 3, 1),),
     (("A", 4, 1),),
-    (("A", 5, 0), ("A", 5, 1),),
-    (),
-    (("A", 8, 0),),
-    (("A", 8, 1), ("A", 10, 0),),
-    (("A", 10, 1),),
-    (("A", 11, 0),),
-    (("A", 11, 1),),
-    (("A", 14, 0),),
-    (("A", 15, 0),),
+    (("A", 6, 0),),
+    (("A", 6, 1),),
+    (("A", 9, 0),),
+    (),
+    (("A", 9, 1),),
+    (),
+    (("A", 12, 0),),
+    (("A", 12, 1),),
+    (("A", 15, 0), ("A", 14, 0),),
     (("A", 14, 1),),
-    (("A", 17, 0), ("A", 15, 1),),
-    (),
-    (("A", 17, 1), ("A", 20, 0),),
-    (),
-    (),
-    (("A", 22, 0), ("A", 20, 1),),
-    (),
-    (("A", 22, 1),),
-    (),
-    (),
-    (("R", 10, 0), ("R", 10, 1),),
+    (("A", 15, 1),),
+    (("A", 17, 0),),
+    (("A", 17, 1),),
+    (("A", 21, 0),),
+    (),
+    (),
+    (("A", 21, 1),),
+    (("A", 25, 0),),
+    (("A", 25, 1),),
+    (("R", 3, 0), ("R", 3, 1),),
+    (),
     (),
     (),
     (("R", 14, 0), ("R", 14, 1),),
     (),
     (),
-    (),
-    (),
-    (),
-    (("R", 22, 0), ("R", 22, 1),),
+    (("R", 9, 0),),
+    (("R", 9, 1),),
+    (),
+    (("R", 21, 0), ("R", 21, 1),),
     (),
 )
-LAST = (("R", 17, 0), ("R", 20, 0), ("R", 20, 1), ("R", 17, 1), ("R", 8, 0), ("R", 8, 1), ("R", 15, 0), ("R", 15, 1), ("R", 4, 0), ("R", 11, 0), ("R", 4, 1), ("R", 11, 1), ("R", 5, 0), ("R", 1, 0), ("R", 5, 1), ("R", 1, 1), ("R", 2, 0), ("R", 2, 1), ("R", 0, 0), ("R", 0, 1),)
+LAST = (("R", 25, 0), ("R", 25, 1), ("R", 15, 0), ("R", 17, 0), ("R", 15, 1), ("R", 17, 1), ("R", 4, 0), ("R", 4, 1), ("R", 12, 0), ("R", 12, 1), ("R", 6, 0), ("R", 1, 0), ("R", 6, 1), ("R", 1, 1), ("R", 2, 0), ("R", 2, 1), ("R", 0, 0), ("R", 0, 1),)
 
 DIRS = ((0, 1), (0, -1), (1, 0), (-1, 0))
 INNER = [k for k in range(CHIPS) if NODES[k][4]]
@@ -108,37 +107,12 @@
 KIDS = {k: [c for c in range(CHIPS) if NODES[c][2] == k] for k in range(CHIPS)}
 
 
-def _sources():
-    rows = np.zeros((CHIPS, 2, 3 * CHIPS), np.int32)
-    goal = np.zeros((CHIPS, 2, 3 * CHIPS), np.int32)
-    for y in range(NY):
-        for z in range(NZ):
-            for core in range(2):
-                out, aim = [], []
-                for c in range(2):
-                    sign = 1 - 2 * c
-                    for dy, dz, *_ in NODES:
-                        out.append((z - sign * dz) % NZ * 2 * NY + (y - sign * dy) % NY * 2 + c)
-                        aim.append(z * NY + y)
-                sign = 1 - 2 * core
-                for dy, dz, parent, way, _ in NODES:
-                    step = DIRS[way] if parent >= 0 else (0, 0)
-                    py, pz = y + sign * step[0], z + sign * step[1]
-                    out.append((pz - sign * dz) % NZ * 2 * NY + (py - sign * dy) % NY * 2 + core)
-                    aim.append(pz % NZ * NY + py % NY)
-                rows[y * NZ + z, core], goal[y * NZ + z, core] = out, aim
-    return rows, goal
-
-
-SOURCE, GOAL = _sources()
-
-
 def tree_kernel(
-    ku_ref, lb_ref, bid_ref, scale_ref, kid_ref, utter_ref, lab_ref, intents_ref,
-    gu_ref, con_ref,
-    ag, outer, stage, aglab, rsin, rep, w, ucur, usel, labsel, part, recv, gs, gown, gbuf, cst,
+    req_ref, home_ref, lab_ref, utter_ref, intents_ref,
+    gu_ref, con_ref, tabs_ref,
+    ag, outer, stage, aglab, rsin, rep, w, ucur, usel, labsel, part, recv, gs, gown, gbuf, cst, reqs, homes, tab, rows_ref,
     sem_in, sem_w, ag_send, ag_recv, out_send, out_recv, lab_send, lab_recv, rs_send, rs_recv, rep_send, rep_recv,
-    part_send, part_recv, gs_send, gs_recv, con_send, con_recv, con_loc, sem_out,
+    part_send, part_recv, gs_send, gs_recv, con_send, con_recv, con_loc, sem_out, sem_tab,
 ):
     z = lax.axis_index("dp")
     cl = lax.axis_index("cls")
@@ -209,12 +183,10 @@
         return pltpu.make_async_copy(ag.at[0, piece], gu_ref.at[piece], sem_out.at[h])
 
     own_u = pltpu.make_async_copy(utter_ref, ag.at[0], sem_in.at[0])
-    own_l = pltpu.make_async_copy(lab_ref, aglab.at[0], sem_in.at[1])
     own_w = pltpu.make_async_copy(intents_ref, w.at[pl.ds(core * BLK_DEV, BLK_DEV)], sem_in.at[2])
     far_w = remote(intents_ref, w.at[pl.ds(core * BLK_DEV, BLK_DEV)], sem_w.at[0], sem_w.at[1], other)
     far_w_in = remote(intents_ref, w.at[pl.ds((1 - core) * BLK_DEV, BLK_DEV)], sem_w.at[0], sem_w.at[1], other)
     own_u.start()
-    own_l.start()
     own_w.start()
 
     barrier = pltpu.get_barrier_semaphore()
@@ -222,8 +194,14 @@
         pl.semaphore_signal(barrier, inc=1, device_id=device, device_id_type=MESH)
     pl.semaphore_wait(barrier, 8)
     own_u.wait()
-    own_l.wait()
+    for k in range(2):
+        for i in range(UBD):
+            aglab[0, k * UBD + i:k * UBD + i + 1] = lab_ref[k:k + 1, i * UB:(i + 1) * UB]
     far_w.start()
+
+    tab_near = pltpu.make_async_copy(tab.at[pl.ds(0, CHIPS)], tabs_ref.at[core], sem_tab.at[1])
+    tab_far = remote(tab.at[pl.ds(0, CHIPS)], tabs_ref.at[core], sem_tab.at[2], sem_tab.at[3], other)
+    tab_in = remote(tab.at[pl.ds(0, CHIPS)], tabs_ref.at[1 - core], sem_tab.at[2], sem_tab.at[3], other)
 
     def pass_on(k, h):
         if k > 0:
@@ -244,17 +222,83 @@
             for c in KIDS[k]:
                 if not NODES[c][4]:
                     for s in range(SLOTS):
-                        stage[SPOT[c], s] = ucur[kid_ref[c * SLOTS + s]]
+                        stage[SPOT[c], s] = ucur[block_of(CHIPS + c, s)]
                     out_copy(c).start()
                     lab_copy(c).start()
             for s in range(SLOTS):
-                usel[d, s] = ucur[ku_ref[k * SLOTS + s]]
+                usel[d, s] = ucur[block_of(k, s)]
         else:
             out_copy(k).wait_recv()
             lab_copy(k).wait_recv()
             for s in range(SLOTS):
                 usel[d, s] = outer[SPOT[k], s]
 
+    def block_of(k, s):
+        return rows_ref[k, s] % 8
+
+    def place_of(k, s):
+        return rows_ref[k, s] // 8 % 128
+
+    def make_plan():
+        lanes = 128
+        for k in range(CHIPS):
+            dy, dz = NODES[k][:2]
+            row = (z + NZ - sign * dz) % NZ * 2 * NY + (y + NY - sign * dy) % NY * 2 + core
+            reqs[k:k + 1] = req_ref[pl.ds(row, 1)]
+        table = home_ref[...]
+        high = (table // 64).astype(jnp.float32).astype(jnp.bfloat16)
+        low = (table % 64).astype(jnp.float32).astype(jnp.bfloat16)
+        tall = lax.broadcasted_iota(jnp.int32, (lanes, lanes), 0)
+        for k in range(CHIPS):
+            ids = reqs[k:k + 1]
+            pick_hi = (tall[:32] == ids // lanes).astype(jnp.float32).astype(jnp.bfloat16)
+            pick_lo = tall == ids % lanes
+            contract = (((0,), (0,)), ((), ()))
+            a = lax.dot_general(high, pick_hi, contract, preferred_element_type=jnp.float32)
+            b = lax.dot_general(low, pick_hi, contract, preferred_element_type=jnp.float32)
+            home = jnp.sum(jnp.where(pick_lo, a * 64.0 + b, 0.0), axis=0, keepdims=True)
+            homes[k:k + 1] = jnp.where(ids >= 0, home.astype(jnp.int32), -1)
+        here = z * NY + y
+        codes = []
+        for dy, dz in DIRS:
+            codes.append((z + NZ + sign * dz) % NZ * NY + (y + NY + sign * dy) % NY)
+        for k in range(CHIPS):
+            parent, way = NODES[k][2:4]
+            if parent >= 0:
+                homes[CHIPS + k:CHIPS + k + 1] = homes[parent:parent + 1] + (here - codes[way]) * 2 * BLK_DEV
+                reqs[CHIPS + k:CHIPS + k + 1] = reqs[parent:parent + 1]
+            else:
+                homes[CHIPS + k:CHIPS + k + 1] = jnp.full((1, lanes), -1, jnp.int32)
+                reqs[CHIPS + k:CHIPS + k + 1] = jnp.full((1, lanes), -1, jnp.int32)
+        ids, home = reqs[...], homes[...]
+        lane = lax.broadcasted_iota(jnp.int32, ids.shape, 1)
+        at = lane.astype(jnp.float32)
+        packed = jnp.zeros(ids.shape, jnp.int32)
+
+        def total(v):
+            return jnp.sum(v.astype(jnp.float32), axis=1, keepdims=True).astype(jnp.int32)
+
+        for o in range(2):
+            base = here * 2 * BLK_DEV + o * BLK_DEV
+            mine = (ids >= 0) & (home >= base) & (home < base + BLK_DEV)
+            first = jnp.min(jnp.where(mine, at, 1000.0), axis=1, keepdims=True).astype(jnp.int32)
+            last = jnp.max(jnp.where(mine, at, -1.0), axis=1, keepdims=True).astype(jnp.int32)
+            for s, (entry, valid) in enumerate(((first, last >= 0), (last, last > first))):
+                hot = mine & (lane == entry)
+                block = entry // MOST
+                place = total(jnp.where(hot, home - here * 2 * BLK_DEV, 0))
+                name = total(jnp.where(hot, ids, 0))
+                listed = total(jnp.where((ids >= 0) & (lane // MOST == block), 1, 0))
+                value = block + 8 * place + 1024 * listed + 32768 * name
+                value = jnp.where(valid, value, 0)
+                packed = packed + jnp.where(lane == 2 * o + s, value, 0)
+        tab[...] = packed
+        fill = pltpu.make_async_copy(tab, rows_ref, sem_tab.at[0])
+        fill.start()
+        tab_near.start()
+        tab_far.start()
+        fill.wait()
+
     def scores(n):
         d = n % DEPTH
 
@@ -263,14 +307,14 @@
             for o in range(1, 4):
                 part_copy(n, o).wait_send()
 
-        mine = ku_ref[n * SLOTS + x]
+        mine = block_of(n, x)
         rows = lax.broadcasted_iota(jnp.int32, (UBD, UB), 0)
         for k in range(2):
             labs = aglab[n, k * UBD:(k + 1) * UBD]
             labsel[d, k:k + 1] = jnp.sum(jnp.where(rows == mine, labs, 0), axis=0, keepdims=True)
         for s in range(SLOTS):
             part[d, s] = lax.dot_general(
-                w[lb_ref[n * SLOTS + s]], usel[d, s], (((1,), (1,)), ((), ())),
+                w[place_of(n, s)], usel[d, s], (((1,), (1,)), ((), ())),
                 preferred_element_type=jnp.float32).astype(part.dtype)
         for o in range(1, 4):
             part_copy(n, o).start()
@@ -288,10 +332,12 @@
             part_copy(m, o).wait_recv()
             total = total + recv[d, o - 1].astype(jnp.float32)
         logits = GAMMA * total
-        ids = lax.broadcasted_iota(jnp.int32, (BLK, UB), 0) + bid_ref[m * SLOTS + x] * BLK
+        ids = lax.broadcasted_iota(jnp.int32, (BLK, UB), 0) + (rows_ref[m, x] // 32768) * BLK
         hit = (ids == labsel[d, 0:1]) | (ids == labsel[d, 1:2])
         slope = jax.nn.sigmoid(jnp.where(hit, MARGIN - logits, logits + MARGIN))
-        slope = jnp.where(hit, -slope, slope) * scale_ref[m * SLOTS + x]
+        listed = jnp.full((1, UB), rows_ref[m, x] // 1024 % 32, jnp.int32).astype(jnp.float32)
+        scale = jnp.where(listed > 0, GAMMA / jnp.maximum(listed, 1.0), 0.0)
+        slope = jnp.where(hit, -slope, slope) * scale
         gs[d, x] = slope.astype(jnp.bfloat16)
         for o in range(1, 4):
             gs_copy(m, o).start()
@@ -311,7 +357,7 @@
             slope = gs[d, s]
             cst[e, s] = jnp.dot(slope, usel[d, s], preferred_element_type=jnp.float32).astype(jnp.bfloat16)
             gown[s] = lax.dot_general(
-                slope, w[lb_ref[m * SLOTS + s]], (((0,), (0,)), ((), ())),
+                slope, w[place_of(m, s)], (((0,), (0,)), ((), ())),
                 preferred_element_type=jnp.float32)
         con_far(m).start()
         con_near(m).start()
@@ -341,10 +387,10 @@
             rows = pl.ds(pl.multiple_of(i % tiles * ROWS, ROWS), ROWS)
             total = jnp.zeros((ROWS, ag.shape[3]), jnp.float32)
             for s in range(SLOTS):
-                total = total + gbuf[SPOT[k], s, rows] * (ku_ref[k * SLOTS + s] == j).astype(jnp.float32)
+                total = total + gbuf[SPOT[k], s, rows] * (block_of(k, s) == j).astype(jnp.float32)
             for c in outer_kids:
                 for s in range(SLOTS):
-                    share = (kid_ref[c * SLOTS + s] == j).astype(jnp.float32)
+                    share = (block_of(CHIPS + c, s) == j).astype(jnp.float32)
                     total = total + rep[SPOT[c], s, rows].astype(jnp.float32) * share
             for c in inner:
                 total = total + rsin[SPOT[c], j, rows].astype(jnp.float32)
@@ -369,7 +415,8 @@
             if k < CHIPS or TASKS[k]:
                 @pl.when(n == k)
                 def _():
-                    do(TASKS[k])
+                    if k > 0:
+                        do(TASKS[k])
                     if k < CHIPS:
                         pick(k)
                     if k == 0:
@@ -394,6 +441,8 @@
                 keep(k)
         return carry
 
+    do(TASKS[0])
+    make_plan()
     lax.fori_loop(0, CHIPS + LAG_GRAD, step, 0)
     do(LAST)
 
@@ -419,16 +468,19 @@
         con_far(n).wait_send()
         con_near(n).wait()
     far_w.wait_send()
+    tab_near.wait()
+    tab_far.wait_send()
+    tab_in.wait_recv()
     for h in range(PARTS):
         out_dma(h).wait()
 
 
-def tree(ku, lb, bid, scale, kid, utter, labs, intents):
+def tree(req, home, labs, utter, intents):
     width = intents.shape[2]
     block = (UB, width)
     dma = pltpu.SemaphoreType.DMA
     anyspace = pl.BlockSpec(memory_space=pl.ANY)
-    smem = pl.BlockSpec(memory_space=pltpu.SMEM)
+    vmem = pl.BlockSpec(memory_space=pltpu.VMEM)
     ni, no = len(INNER), len(OUTER)
     bf16 = jnp.bfloat16
     return pl.pallas_call(
@@ -436,9 +488,10 @@
         out_shape=(
             jax.ShapeDtypeStruct((UBD,) + block, bf16),
             jax.ShapeDtypeStruct((2, CHIPS, 2) + block, bf16),
+            jax.ShapeDtypeStruct((2, CHIPS, 128), jnp.int32),
         ),
-        in_specs=[smem] * 5 + [anyspace] * 3,
-        out_specs=(anyspace, anyspace),
+        in_specs=[vmem] * 3 + [anyspace] * 2,
+        out_specs=(anyspace, anyspace, anyspace),
         scratch_shapes=[
             pltpu.VMEM((ni, UBD) + block, bf16),
             pltpu.VMEM((no, SLOTS) + block, bf16),
@@ -456,24 +509,29 @@
             pltpu.VMEM((SLOTS,) + block, jnp.float32),
             pltpu.VMEM((ni, SLOTS) + block, jnp.float32),
             pltpu.VMEM((CON_DEPTH, SLOTS) + block, bf16),
+            pltpu.VMEM((2 * CHIPS, 128), jnp.int32),
+            pltpu.VMEM((2 * CHIPS, 128), jnp.int32),
+            pltpu.VMEM((2 * CHIPS, 128), jnp.int32),
+            pltpu.SMEM((2 * CHIPS, 128), jnp.int32),
             dma((3,)), dma((2,)),
             dma((ni, PARTS)), dma((ni, PARTS)), dma((no,)), dma((no,)), dma((CHIPS,)), dma((CHIPS,)),
             dma((ni, PARTS)), dma((ni, PARTS)), dma((no,)), dma((no,)),
             dma((DEPTH, 3)), dma((DEPTH, 3)), dma((DEPTH, 3)), dma((DEPTH, 3)),
-            dma((CON_DEPTH,)), dma((CHIPS,)), dma((CON_DEPTH,)), dma((PARTS,)),
+            dma((CON_DEPTH,)), dma((CHIPS,)), dma((CON_DEPTH,)), dma((PARTS,)), dma((4,)),
         ],
         compiler_params=pltpu.CompilerParams(
             collective_id=0, has_side_effects=True, vmem_limit_bytes=60 * 1024 * 1024),
         name="tree",
-    )(ku, lb, bid, scale, kid, utter, labs, intents)
+    )(req, home, labs, utter, intents)
 
 
 SCORE = jnp.bfloat16
 CHUNK = 16
 
 
-def gather_kernel(lb_ref, con_ref, out_ref, con, acc, res, sem_in, sem_out):
+def gather_kernel(tabs_ref, con_ref, out_ref, con, acc, res, sem_in, sem_out):
     count = con.shape[0]
+    core = lax.axis_index("cls") % 2
 
     def load(i):
         piece = pl.ds(i * CHUNK, CHUNK)
@@ -486,15 +544,20 @@
     for i in range(count // CHUNK):
         load(i).start()
     acc[...] = jnp.zeros_like(acc)
-    for i in range(count // CHUNK):
+
+    def chunk(i, carry):
         load(i).wait()
-
-        def add(k, carry):
-            b = lb_ref[i * CHUNK + k]
-            acc[b] = acc[b] + con[i * CHUNK + k].astype(jnp.float32)
-            return carry
-
-        lax.fori_loop(0, CHUNK, add, 0)
+        for k in range(CHUNK):
+            slot = i * CHUNK + k
+            packed = tabs_ref[slot // (2 * CHIPS), slot // 2 % CHIPS, core * 2 + k % 2]
+
+            @pl.when(packed > 0)
+            def _():
+                b = packed // 8 % BLK_DEV
+                acc[b] = acc[b] + con[slot].astype(jnp.float32)
+        return carry
+
+    lax.fori_loop(0, count // CHUNK, chunk, 0)
     for i in range(BLK_DEV // CHUNK):
         piece = pl.ds(i * CHUNK, CHUNK)
         res[piece] = acc[piece].astype(res.dtype)
@@ -503,7 +566,7 @@
         store(i).wait()
 
 
-def gather(lb, con):
+def gather(tabs, con):
     count, width = con.shape[0], con.shape[2]
     dma = pltpu.SemaphoreType.DMA
     return pl.pallas_call(
@@ -519,59 +582,15 @@
         out_shape=jax.ShapeDtypeStruct((BLK_DEV, BLK, width), jnp.bfloat16),
         compiler_params=pltpu.CompilerParams(vmem_limit_bytes=60 * 1024 * 1024),
         name="sum_blocks",
-    )(lb, con)
-
-
-def plan(req_blocks, req_count, block_home):
-    z = lax.axis_index("dp")
-    cl = lax.axis_index("cls")
-    chip, core = (cl // 2) * NZ + z, cl % 2
-    rows = lax.dynamic_slice(jnp.asarray(SOURCE), (chip, core, 0), (1, 1, 3 * CHIPS)).reshape(3 * CHIPS)
-    goal = lax.dynamic_slice(jnp.asarray(GOAL), (chip, core, 0), (1, 1, 3 * CHIPS)).reshape(3 * CHIPS)
-    entries = UBD * MOST
-    wide = 64
-    req = req_blocks.reshape(2 * CHIPS * entries)
-    spread = (jnp.arange(wide)[:, None] == (req // wide)[None, :]).astype(jnp.bfloat16)
-    table = block_home.reshape(wide, wide).T
-    halves = jnp.concatenate([table // wide, table % wide], axis=0).astype(jnp.bfloat16)
-    found = jnp.dot(halves, spread, preferred_element_type=jnp.float32).reshape(2, wide, -1)
-    low = jnp.arange(wide)[:, None] == (req % wide)[None, :]
-    found = jnp.sum(jnp.where(low[None], found, 0.0), axis=1).astype(jnp.int32)
-    home = jnp.where(req >= 0, found[0] * wide + found[1], -1)
-    req = req.reshape(2 * CHIPS, entries)[rows]
-    home = home.reshape(2 * CHIPS, entries)[rows]
-    count = req_count.reshape(2 * CHIPS, UBD)[rows]
-    at = jnp.arange(entries)[None, None, :]
-    side = goal[:, None] * 2 + jnp.arange(2)[None, :]
-    mine = (home[:, None, :] >= 0) & (home[:, None, :] // BLK_DEV == side[:, :, None])
-    first = jnp.min(jnp.where(mine, at, entries), axis=2)
-    last = jnp.max(jnp.where(mine, at, -1), axis=2)
-    entry = jnp.stack([first, last], axis=2)
-    valid = jnp.stack([last >= 0, last > first], axis=2)
-    hot = (at[..., None, :] == entry[..., None]) & valid[..., None]
-    lb = jnp.sum(jnp.where(hot, home[:, None, None, :] % (2 * BLK_DEV), 0), axis=3)
-    bid = jnp.sum(jnp.where(hot, req[:, None, None, :], 0), axis=3)
-    ku = jnp.where(valid, entry // MOST, 0)
-    listed = jnp.sum(jnp.where(ku[..., None] == jnp.arange(UBD), count[:, None, None, :], 0), axis=3)
-    scale = jnp.where(valid, GAMMA / listed.astype(jnp.float32), 0.0)
-    return ku, lb, bid, scale
+    )(tabs, con)
 
 
 def shards(utter, intents, req_blocks, req_count, block_home, labels):
-    core = lax.axis_index("cls") % 2
     width = intents.shape[1]
-    ku, lb, bid, scale = plan(req_blocks, req_count, block_home)
-
-    def row(t, c):
-        return lax.dynamic_slice_in_dim(t.reshape(3 * CHIPS * SLOTS), c * CHIPS * SLOTS, CHIPS * SLOTS)
-
-    labs = labels.reshape(UBD, UB, 2).transpose(2, 0, 1).reshape(2 * UBD, UB)
-    grad_utter, con = tree(
-        row(ku, core), row(lb, core), row(bid, core), row(scale, core), row(ku, 2),
-        utter.reshape(UBD, UB, width), labs, intents.reshape(BLK_DEV, BLK, width))
-    near = lax.dynamic_index_in_dim(
-        lb[:2 * CHIPS].reshape(2 * CHIPS, 2, 2), core, 1, keepdims=False).reshape(4 * CHIPS) % BLK_DEV
-    grad_intents = gather(near, con.reshape(4 * CHIPS, BLK, width))
+    grad_utter, con, tabs = tree(
+        req_blocks.reshape(2 * CHIPS, UBD * MOST), block_home.reshape(-1, 128), labels.T,
+        utter.reshape(UBD, UB, width), intents.reshape(BLK_DEV, BLK, width))
+    grad_intents = gather(tabs, con.reshape(4 * CHIPS, BLK, width))
     return grad_utter.reshape(UBD * UB, width), grad_intents.reshape(BLK_DEV * BLK, width)
 
 

time: 190 us -> 173 us (0.911)
  local copies, waits for them, and re-layouts: 11.8 us -> 2.43 us
  other arithmetic: 3.08 us -> 0 us
    pallas_call x1, Pallas kernels: 165 us -> 161 us  [tree(): pl.pallas_call(tree_kernel, out_shape=(jax.ShapeDtypeStruct((UBD,) + bloc...]
    dynamic_slice x9 -> x0, local copies, waits for them, and re-layouts: 3.4 us -> none  [the longest x7 3.3 us: row(): lax.dynamic_slice_in_dim(t.reshape(3 * CHIPS * SLOTS), c * CHIPS * SLOTS,...]
    pallas_call x1, Pallas kernels: 6.65 us -> 8.86 us  [gather(): pl.pallas_call(gather_kernel, in_specs=[pl.BlockSpec(memory_space=pltpu.S...]
    gather x4 -> x0, local copies, waits for them, and re-layouts: 1.92 us -> none  [the longest x2 0.67 us: plan(): count = req_count.reshape(2 * CHIPS, UBD)[rows]]
where the time goes in v3:
time: 173 us
  Pallas kernels  170 us (98%)
  local copies, waits for them, and re-layouts  2.43 us (1%)
    pallas_call x1, Pallas kernels, tree(): pl.pallas_call(tree_kernel, out_shape=(jax.ShapeDtypeStruct((UBD,) + bloc...  161 us
    pallas_call x1, Pallas kernels, gather(): pl.pallas_call(gather_kernel, in_specs=[pl.BlockSpec(memory_space=pltpu.S...  8.86 us

profile of v3, /device:TPU:64, one launch (start us, length us, event | category | flops | bytes accessed | tf_op | source)
XLA Modules:
  0.0 172.8 jit_solution(14928445505674477121)
XLA Ops:
  0.6 0.9 copy.8
  1.5 0.7 reshape.25.req_ref
  2.3 160.8 %tree.1 = (bf16[8,128,256]{2,1,0:T(8,128)(2,1)}, bf16[2,32,2,128,256]{4,3,2,1,0:T(8,128)(2,1)}, s32[2,32,128]{2,1,0:T(8,128)}) custom-call(s32[64,128]{1,0:T(8,128)} %reshape.25.req_ref, s32[32,128]{1,0:T(8,128)} %bitcast.12, s32[2,1024]{1,0:T(2,128)} %bitcast.13, bf16[8,128,256]{2,1,0:T(8,128)(2,1)} %bitcast.10, bf16[64,128,256]{2,1,0:T(8,128)(2,1)} %bitcast.9), custom_call_target="tpu_custom_call" | custom-call | tf_op jit(solution)/shard_map/tree/pallas_call | solution.py:486
  163.1 0.0 copy-start
  163.1 8.9 %sum_blocks.1 = bf16[64,128,256]{2,1,0:T(8,128)(2,1)} custom-call(s32[2,32,128]{2,1,0:T(8,128)} %get-tuple-element.6.tabs_ref, bf16[128,128,256]{2,1,0:T(8,128)(2,1)} %bitcast.7), custom_call_target="tpu_custom_call" | custom-call | tf_op jit(solution)/shard_map/sum_blocks/pallas_call | solution.py:572
  172.0 0.0 copy-done
  172.0 0.8 copy.10
Async XLA Ops:
  163.1 8.9 %copy-start = (bf16[8,128,256]{2,1,0:T(8,128)(2,1)S(1)}, bf16[8,128,256]{2,1,0:T(8,128)(2,1)}, u32[]{:S(2)}) copy-start(bf16[8,128,256]{2,1,0:T(8,128)(2,1)} %get-tuple-element.5) | copy-start | bytes 1572868

commit v4 on v3

--- a/solution.py
+++ b/solution.py
@@ -110,7 +110,7 @@
 def tree_kernel(
     req_ref, home_ref, lab_ref, utter_ref, intents_ref,
     gu_ref, con_ref, tabs_ref,
-    ag, outer, stage, aglab, rsin, rep, w, ucur, usel, labsel, part, recv, gs, gown, gbuf, cst, reqs, homes, tab, rows_ref,
+    ag, outer, stage, aglab, rsin, rep, w, ucur, usel, labsel, part, recv, gs, gown, gbuf, cst, lists, eight, reqs, homes, tab, rows_ref,
     sem_in, sem_w, ag_send, ag_recv, out_send, out_recv, lab_send, lab_recv, rs_send, rs_recv, rep_send, rep_recv,
     part_send, part_recv, gs_send, gs_recv, con_send, con_recv, con_loc, sem_out, sem_tab,
 ):
@@ -241,10 +241,19 @@
 
     def make_plan():
         lanes = 128
+        for q in range(lists.shape[0] // lanes):
+            columns = req_ref[:, q * lanes:(q + 1) * lanes]
+            lists[q * lanes:(q + 1) * lanes] = jnp.concatenate(
+                [columns, jnp.zeros((lanes - MOST, lanes), jnp.int32)], axis=0).T
         for k in range(CHIPS):
             dy, dz = NODES[k][:2]
             row = (z + NZ - sign * dz) % NZ * 2 * NY + (y + NY - sign * dy) % NY * 2 + core
-            reqs[k:k + 1] = req_ref[pl.ds(row, 1)]
+            eight[k * UBD:(k + 1) * UBD] = lists[pl.ds(pl.multiple_of(row * UBD, UBD), UBD)]
+        spot = lax.broadcasted_iota(jnp.int32, (CHIPS, lanes), 1) // MOST
+        row = jnp.zeros((CHIPS, lanes), jnp.int32)
+        for i in range(UBD):
+            row = jnp.where(spot == i, pltpu.roll(eight[pl.ds(i, CHIPS, stride=UBD)], i * MOST, 1), row)
+        reqs[0:CHIPS] = row
         table = home_ref[...]
         high = (table // 64).astype(jnp.float32).astype(jnp.bfloat16)
         low = (table % 64).astype(jnp.float32).astype(jnp.bfloat16)
@@ -509,6 +518,8 @@
             pltpu.VMEM((SLOTS,) + block, jnp.float32),
             pltpu.VMEM((ni, SLOTS) + block, jnp.float32),
             pltpu.VMEM((CON_DEPTH, SLOTS) + block, bf16),
+            pltpu.VMEM((2 * CHIPS * UBD, 128), jnp.int32),
+            pltpu.VMEM((CHIPS * UBD, 128), jnp.int32),
             pltpu.VMEM((2 * CHIPS, 128), jnp.int32),
             pltpu.VMEM((2 * CHIPS, 128), jnp.int32),
             pltpu.VMEM((2 * CHIPS, 128), jnp.int32),
@@ -529,7 +540,7 @@
 CHUNK = 16
 
 
-def gather_kernel(tabs_ref, con_ref, out_ref, con, acc, res, sem_in, sem_out):
+def gather_kernel(tabs_ref, con_ref, gu_ref, out_ref, gu_out, con, acc, res, gu, sem_in, sem_out, sem_gu):
     count = con.shape[0]
     core = lax.axis_index("cls") % 2
 
@@ -543,54 +554,60 @@
 
     for i in range(count // CHUNK):
         load(i).start()
+    gu_load = pltpu.make_async_copy(gu_ref, gu, sem_gu.at[0])
+    gu_store = pltpu.make_async_copy(gu, gu_out, sem_gu.at[1])
+    gu_load.start()
     acc[...] = jnp.zeros_like(acc)
 
     def chunk(i, carry):
         load(i).wait()
+        half, row = i // (2 * CHIPS // CHUNK), i % (2 * CHIPS // CHUNK) * (CHUNK // 2)
         for k in range(CHUNK):
-            slot = i * CHUNK + k
-            packed = tabs_ref[slot // (2 * CHIPS), slot // 2 % CHIPS, core * 2 + k % 2]
-
-            @pl.when(packed > 0)
-            def _():
-                b = packed // 8 % BLK_DEV
-                acc[b] = acc[b] + con[slot].astype(jnp.float32)
+            b = tabs_ref[half, row + k // 2, core * 2 + k % 2] // 8 % BLK_DEV
+            acc[b] = acc[b] + con[i * CHUNK + k].astype(jnp.float32)
         return carry
 
     lax.fori_loop(0, count // CHUNK, chunk, 0)
+    gu_load.wait()
+    gu_store.start()
     for i in range(BLK_DEV // CHUNK):
         piece = pl.ds(i * CHUNK, CHUNK)
         res[piece] = acc[piece].astype(res.dtype)
         store(i).start()
     for i in range(BLK_DEV // CHUNK):
         store(i).wait()
-
-
-def gather(tabs, con):
+    gu_store.wait()
+
+
+def gather(tabs, con, grad_utter):
     count, width = con.shape[0], con.shape[2]
     dma = pltpu.SemaphoreType.DMA
     return pl.pallas_call(
         gather_kernel,
-        in_specs=[pl.BlockSpec(memory_space=pltpu.SMEM), pl.BlockSpec(memory_space=pl.ANY)],
-        out_specs=pl.BlockSpec(memory_space=pl.ANY),
+        in_specs=[pl.BlockSpec(memory_space=pltpu.SMEM)] + [pl.BlockSpec(memory_space=pl.ANY)] * 2,
+        out_specs=(pl.BlockSpec(memory_space=pl.ANY),) * 2,
         scratch_shapes=[
             pltpu.VMEM((count, BLK, width), jnp.bfloat16),
             pltpu.VMEM((BLK_DEV, BLK, width), jnp.float32),
             pltpu.VMEM((BLK_DEV, BLK, width), jnp.bfloat16),
-            dma((count // CHUNK,)), dma((BLK_DEV // CHUNK,)),
+            pltpu.VMEM(grad_utter.shape, grad_utter.dtype),
+            dma((count // CHUNK,)), dma((BLK_DEV // CHUNK,)), dma((2,)),
         ],
-        out_shape=jax.ShapeDtypeStruct((BLK_DEV, BLK, width), jnp.bfloat16),
+        out_shape=(
+            jax.ShapeDtypeStruct((BLK_DEV, BLK, width), jnp.bfloat16),
+            jax.ShapeDtypeStruct(grad_utter.shape, grad_utter.dtype),
+        ),
         compiler_params=pltpu.CompilerParams(vmem_limit_bytes=60 * 1024 * 1024),
         name="sum_blocks",
-    )(tabs, con)
+    )(tabs, con, grad_utter)
 
 
 def shards(utter, intents, req_blocks, req_count, block_home, labels):
     width = intents.shape[1]
     grad_utter, con, tabs = tree(
-        req_blocks.reshape(2 * CHIPS, UBD * MOST), block_home.reshape(-1, 128), labels.T,
+        req_blocks.T, block_home.reshape(-1, 128), labels.T,
         utter.reshape(UBD, UB, width), intents.reshape(BLK_DEV, BLK, width))
-    grad_intents = gather(tabs, con.reshape(4 * CHIPS, BLK, width))
+    grad_intents, grad_utter = gather(tabs, con.reshape(4 * CHIPS, BLK, width), grad_utter)
     return grad_utter.reshape(UBD * UB, width), grad_intents.reshape(BLK_DEV * BLK, width)
 
 

time: 173 us -> 169 us (0.977)
  local copies, waits for them, and re-layouts: 2.43 us -> 0 us
  Pallas kernels: 170 us -> 168 us
    pallas_call x1, Pallas kernels: 8.86 us -> 7.11 us  [gather(): pl.pallas_call(gather_kernel, in_specs=[pl.BlockSpec(memory_space=pltpu.S...]
where the time goes in v4:
time: 169 us
  Pallas kernels  168 us (99%)
    pallas_call x1, Pallas kernels, tree(): pl.pallas_call(tree_kernel, out_shape=(jax.ShapeDtypeStruct((UBD,) + bloc...  161 us
    pallas_call x1, Pallas kernels, gather(): pl.pallas_call(gather_kernel, in_specs=[pl.BlockSpec(memory_space=pltpu.S...  7.11 us

profile of v4, /device:TPU:64, one launch (start us, length us, event | category | flops | bytes accessed | tf_op | source)
XLA Modules:
  0.0 169.0 jit_solution(1550219815751064927)
XLA Ops:
  0.6 161.2 %tree.1 = (bf16[8,128,256]{2,1,0:T(8,128)(2,1)}, bf16[2,32,2,128,256]{4,3,2,1,0:T(8,128)(2,1)}, s32[2,32,128]{2,1,0:T(8,128)}) custom-call(s32[16,512]{1,0:T(8,128)} %bitcast.11, s32[32,128]{1,0:T(8,128)} %bitcast.12, s32[2,1024]{1,0:T(2,128)} %bitcast.13, bf16[8,128,256]{2,1,0:T(8,128)(2,1)} %bitcast.10, bf16[64,128,256]{2,1,0:T(8,128)(2,1)} %bitcast.9), custom_call_target="tpu_custom_call" | custom-call | tf_op jit(solution)/shard_map/tree/pallas_call | solution.py:495
  161.9 7.1 %sum_blocks.1 = (bf16[64,128,256]{2,1,0:T(8,128)(2,1)}, bf16[8,128,256]{2,1,0:T(8,128)(2,1)}) custom-call(s32[2,32,128]{2,1,0:T(8,128)} %get-tuple-element.7.tabs_ref, bf16[128,128,256]{2,1,0:T(8,128)(2,1)} %bitcast.8, bf16[8,128,256]{2,1,0:T(8,128)(2,1)} %get-tuple-element.9.gu_ref), custom_call_target="tpu_custom_call" | custom-call | tf_op jit(solution)/shard_map/sum_blocks/pallas_call | solution.py:585

commit v5 on v4

--- a/solution.py
+++ b/solution.py
@@ -98,6 +98,7 @@
     (),
 )
 LAST = (("R", 25, 0), ("R", 25, 1), ("R", 15, 0), ("R", 17, 0), ("R", 15, 1), ("R", 17, 1), ("R", 4, 0), ("R", 4, 1), ("R", 12, 0), ("R", 12, 1), ("R", 6, 0), ("R", 1, 0), ("R", 6, 1), ("R", 1, 1), ("R", 2, 0), ("R", 2, 1), ("R", 0, 0), ("R", 0, 1),)
+EARLY = ()
 
 DIRS = ((0, 1), (0, -1), (1, 0), (-1, 0))
 INNER = [k for k in range(CHIPS) if NODES[k][4]]
@@ -429,6 +430,7 @@
                     if k < CHIPS:
                         pick(k)
                     if k == 0:
+                        do(EARLY)
                         own_w.wait()
                         far_w_in.wait_recv()
 
@@ -453,14 +455,11 @@
     do(TASKS[0])
     make_plan()
     lax.fori_loop(0, CHIPS + LAG_GRAD, step, 0)
-    do(LAST)
+    do(LAST[:-2 * PARTS])
 
     for k in range(1, CHIPS):
         lab_copy(k).wait_send()
-        if NODES[k][4]:
-            for h in range(PARTS):
-                rs_copy(k, h).wait_send()
-        else:
+        if not NODES[k][4]:
             out_copy(k).wait_send()
             rep_copy(k).wait_send()
 
@@ -480,6 +479,10 @@
     tab_near.wait()
     tab_far.wait_send()
     tab_in.wait_recv()
+    do(LAST[-2 * PARTS:])
+    for k in INNER[1:]:
+        for h in range(PARTS):
+            rs_copy(k, h).wait_send()
     for h in range(PARTS):
         out_dma(h).wait()
 
@@ -538,9 +541,10 @@
 
 SCORE = jnp.bfloat16
 CHUNK = 16
-
-
-def gather_kernel(tabs_ref, con_ref, gu_ref, out_ref, gu_out, con, acc, res, gu, sem_in, sem_out, sem_gu):
+OUT = 8
+
+
+def gather_kernel(tabs_hbm, con_ref, gu_ref, out_ref, gu_out, tabs_ref, con, acc, res, gu, sem_in, sem_out, sem_gu):
     count = con.shape[0]
     core = lax.axis_index("cls") % 2
 
@@ -549,7 +553,7 @@
         return pltpu.make_async_copy(con_ref.at[piece], con.at[piece], sem_in.at[i])
 
     def store(i):
-        piece = pl.ds(i * CHUNK, CHUNK)
+        piece = pl.ds(i * OUT, OUT)
         return pltpu.make_async_copy(res.at[piece], out_ref.at[piece], sem_out.at[i])
 
     for i in range(count // CHUNK):
@@ -557,7 +561,10 @@
     gu_load = pltpu.make_async_copy(gu_ref, gu, sem_gu.at[0])
     gu_store = pltpu.make_async_copy(gu, gu_out, sem_gu.at[1])
     gu_load.start()
+    tabs_load = pltpu.make_async_copy(tabs_hbm, tabs_ref, sem_gu.at[2])
+    tabs_load.start()
     acc[...] = jnp.zeros_like(acc)
+    tabs_load.wait()
 
     def chunk(i, carry):
         load(i).wait()
@@ -570,11 +577,11 @@
     lax.fori_loop(0, count // CHUNK, chunk, 0)
     gu_load.wait()
     gu_store.start()
-    for i in range(BLK_DEV // CHUNK):
-        piece = pl.ds(i * CHUNK, CHUNK)
+    for i in range(BLK_DEV // OUT):
+        piece = pl.ds(i * OUT, OUT)
         res[piece] = acc[piece].astype(res.dtype)
         store(i).start()
-    for i in range(BLK_DEV // CHUNK):
+    for i in range(BLK_DEV // OUT):
         store(i).wait()
     gu_store.wait()
 
@@ -584,14 +591,15 @@
     dma = pltpu.SemaphoreType.DMA
     return pl.pallas_call(
         gather_kernel,
-        in_specs=[pl.BlockSpec(memory_space=pltpu.SMEM)] + [pl.BlockSpec(memory_space=pl.ANY)] * 2,
+        in_specs=[pl.BlockSpec(memory_space=pl.ANY)] * 3,
         out_specs=(pl.BlockSpec(memory_space=pl.ANY),) * 2,
         scratch_shapes=[
+            pltpu.SMEM(tabs.shape, jnp.int32),
             pltpu.VMEM((count, BLK, width), jnp.bfloat16),
             pltpu.VMEM((BLK_DEV, BLK, width), jnp.float32),
             pltpu.VMEM((BLK_DEV, BLK, width), jnp.bfloat16),
             pltpu.VMEM(grad_utter.shape, grad_utter.dtype),
-            dma((count // CHUNK,)), dma((BLK_DEV // CHUNK,)), dma((2,)),
+            dma((count // CHUNK,)), dma((BLK_DEV // OUT,)), dma((3,)),
         ],
         out_shape=(
             jax.ShapeDtypeStruct((BLK_DEV, BLK, width), jnp.bfloat16),

time: 169 us -> 168 us (level)
  no operation moved by 1% of the time
where the time goes in v5:
time: 168 us
  Pallas kernels  167 us (99%)
    pallas_call x1, Pallas kernels, tree(): pl.pallas_call(tree_kernel, out_shape=(jax.ShapeDtypeStruct((UBD,) + bloc...  161 us
    pallas_call x1, Pallas kernels, gather(): pl.pallas_call(gather_kernel, in_specs=[pl.BlockSpec(memory_space=pl.ANY)...  6.11 us

profile of v5, /device:TPU:64, one launch (start us, length us, event | category | flops | bytes accessed | tf_op | source)
XLA Modules:
  0.0 168.0 jit_solution(1136985804545484868)
XLA Ops:
  0.6 161.2 %tree.1 = (bf16[8,128,256]{2,1,0:T(8,128)(2,1)}, bf16[2,32,2,128,256]{4,3,2,1,0:T(8,128)(2,1)}, s32[2,32,128]{2,1,0:T(8,128)}) custom-call(s32[16,512]{1,0:T(8,128)} %bitcast.11, s32[32,128]{1,0:T(8,128)} %bitcast.12, s32[2,1024]{1,0:T(2,128)} %bitcast.13, bf16[8,128,256]{2,1,0:T(8,128)(2,1)} %bitcast.10, bf16[64,128,256]{2,1,0:T(8,128)(2,1)} %bitcast.9), custom_call_target="tpu_custom_call" | custom-call | tf_op jit(solution)/shard_map/tree/pallas_call | solution.py:498
  161.9 6.1 %sum_blocks.1 = (bf16[64,128,256]{2,1,0:T(8,128)(2,1)}, bf16[8,128,256]{2,1,0:T(8,128)(2,1)}) custom-call(s32[2,32,128]{2,1,0:T(8,128)} %get-tuple-element.7.tabs_hbm, bf16[128,128,256]{2,1,0:T(8,128)(2,1)} %bitcast.8, bf16[8,128,256]{2,1,0:T(8,128)(2,1)} %get-tuple-element.9.gu_ref), custom_call_target="tpu_custom_call" | custom-call | tf_op jit(solution)/shard_map/sum_blocks/pallas_call | solution.py:592

commit v6 on v5

--- a/solution.py
+++ b/solution.py
@@ -522,7 +522,7 @@
             pltpu.VMEM((ni, SLOTS) + block, jnp.float32),
             pltpu.VMEM((CON_DEPTH, SLOTS) + block, bf16),
             pltpu.VMEM((2 * CHIPS * UBD, 128), jnp.int32),
-            pltpu.VMEM((CHIPS * UBD, 128), jnp.int32),
+            pltpu.VMEM((CHIPS * UBD + UBD, 128), jnp.int32),
             pltpu.VMEM((2 * CHIPS, 128), jnp.int32),
             pltpu.VMEM((2 * CHIPS, 128), jnp.int32),
             pltpu.VMEM((2 * CHIPS, 128), jnp.int32),

time: 168 us -> 168 us (level)
  no operation moved by 1% of the time
where the time goes in v6:
time: 168 us
  Pallas kernels  167 us (99%)
    pallas_call x1, Pallas kernels, tree(): pl.pallas_call(tree_kernel, out_shape=(jax.ShapeDtypeStruct((UBD,) + bloc...  161 us
    pallas_call x1, Pallas kernels, gather(): pl.pallas_call(gather_kernel, in_specs=[pl.BlockSpec(memory_space=pl.ANY)...  6.11 us

profile of v6, /device:TPU:64, one launch (start us, length us, event | category | flops | bytes accessed | tf_op | source)
XLA Modules:
  0.0 168.0 jit_solution(18269916440704262366)
XLA Ops:
  0.6 161.2 %tree.1 = (bf16[8,128,256]{2,1,0:T(8,128)(2,1)}, bf16[2,32,2,128,256]{4,3,2,1,0:T(8,128)(2,1)}, s32[2,32,128]{2,1,0:T(8,128)}) custom-call(s32[16,512]{1,0:T(8,128)} %bitcast.11, s32[32,128]{1,0:T(8,128)} %bitcast.12, s32[2,1024]{1,0:T(2,128)} %bitcast.13, bf16[8,128,256]{2,1,0:T(8,128)(2,1)} %bitcast.10, bf16[64,128,256]{2,1,0:T(8,128)(2,1)} %bitcast.9), custom_call_target="tpu_custom_call" | custom-call | tf_op jit(solution)/shard_map/tree/pallas_call | solution.py:498
  161.9 6.1 %sum_blocks.1 = (bf16[64,128,256]{2,1,0:T(8,128)(2,1)}, bf16[8,128,256]{2,1,0:T(8,128)(2,1)}) custom-call(s32[2,32,128]{2,1,0:T(8,128)} %get-tuple-element.7.tabs_hbm, bf16[128,128,256]{2,1,0:T(8,128)(2,1)} %bitcast.8, bf16[8,128,256]{2,1,0:T(8,128)(2,1)} %get-tuple-element.9.gu_ref), custom_call_target="tpu_custom_call" | custom-call | tf_op jit(solution)/shard_map/sum_blocks/pallas_call | solution.py:592
